TPU v7x, 128 devices: a whole 4x4x4 slice. The times are simulated.
128 devices in a mesh: frag: 32 (over y, z, core), aux: 4 (over x).
Axes of the slice: x: 4, y: 4, z: 4, core: 2. Of those that a mesh axis runs over, the one named last changes fastest.
Arguments:
- blocks: bfloat16 [32, 3008, 4096], P('frag', 'aux'), may hold values from -0.0546875 to 0.0546875
- occ_energy: float32 [32, 16], replicated, may hold values from -2 to -0.5
- vir_energy: float32 [32, 256], replicated, may hold values from 0.5 to 3
- occ_count: int32 [32], replicated, may hold values from 8 to 16, as said below
- vir_count: int32 [32], replicated, may hold values from 128 to 256, as said below
- partner_offset: int32 [32], P('frag'), may hold values from 1 to 3, as said below
Outputs:
- pair_energy: float32 [32], P('frag')
- density: float32 [32, 256, 256], P('frag', 'aux')
Inputs may be any that keep to these rules, and one draw needn't show every extreme that they name: `occ_count`: every count lies in 8 to 16, and some fragment holds exactly 16. `vir_count`: every count lies in 128 to 256, and some fragment holds exactly 256. Padded orbitals take no part in any pair. `partner_offset`: partners are 1 to 3 fragments ahead; both ends occur in every draw. A partner at 32 or beyond means the fragment leads no pair.
All inputs are finite; a program needn't handle non-finite values.
Results may differ from a plain program's by a relative error of at most 0.0003.
Values may be sent and summed in bfloat16 or wider, within the bound.
A program may use at most 192 MiB of HBM per device.

v0:
```python
import jax
import jax.numpy as jnp
from jax import lax
from jax.sharding import PartitionSpec as P

REACH = 3


def passed_along(array, axis, by):
    devices = lax.axis_size(axis)
    pairs = [(i, i + by) for i in range(devices) if 0 <= i + by < devices]
    return lax.ppermute(array, axis, pairs)


def on_device(blocks, occ_energy, vir_energy, occ_count, vir_count, partner_offset):
    frag_total = occ_energy.shape[0]
    occ_width = occ_energy.shape[1]
    vir_width = vir_energy.shape[1]
    aux_devices = lax.axis_size("aux")
    occ_local = occ_width // aux_devices
    row_count = occ_local * vir_width
    own_block = blocks[0]
    fragment = lax.axis_index("frag")
    aux_index = lax.axis_index("aux")
    partner_step = partner_offset[0]
    partner = fragment + partner_step
    valid = partner < frag_total
    clipped = jnp.minimum(partner, frag_total - 1)
    window_pieces = [own_block[None]]
    for distance in range(1, REACH + 1):
        window_pieces.append(passed_along(own_block[None], "frag", -distance))
    window_blocks = jnp.concatenate(window_pieces, 0)
    partner_block = lax.dynamic_index_in_dim(window_blocks, partner_step, 0, keepdims=False)
    own_rows = lax.all_to_all(own_block, "aux", split_axis=1, concat_axis=0, tiled=True)
    integrals = lax.dot_general(
        own_rows,
        lax.all_gather(partner_block, "aux", axis=0, tiled=True),
        (((0,), (0,)), ((), ())),
        preferred_element_type=jnp.float32,
    )
    occ_ids = jnp.arange(occ_width, dtype=jnp.int32)
    vir_ids = jnp.arange(vir_width, dtype=jnp.int32)
    local_occ = aux_index * occ_local + jnp.arange(occ_local, dtype=jnp.int32)
    own_occ = lax.dynamic_slice_in_dim(occ_energy[fragment], aux_index * occ_local, occ_local, 0)
    row_energy = (own_occ[:, None] - vir_energy[fragment][None, :]).reshape(row_count)
    col_energy = (occ_energy[clipped][:, None] - vir_energy[clipped][None, :]).reshape(
        occ_width * vir_width
    )
    row_mask = (
        (local_occ < occ_count[fragment])[:, None] & (vir_ids < vir_count[fragment])[None, :]
    ).reshape(row_count)
    col_mask = (
        (occ_ids < occ_count[clipped])[:, None] & (vir_ids < vir_count[clipped])[None, :]
    ).reshape(occ_width * vir_width)
    full_mask = row_mask[:, None] & col_mask[None, :] & valid
    amplitude = jnp.where(
        full_mask, integrals / (row_energy[:, None] + col_energy[None, :]), jnp.float32(0.0)
    )
    energy = lax.psum(jnp.sum(amplitude * integrals), "aux")
    amp_half = amplitude.astype(jnp.bfloat16)
    by_virtual = (
        amp_half.reshape(occ_local, vir_width, occ_width * vir_width)
        .transpose(1, 0, 2)
        .reshape(vir_width, occ_local * occ_width * vir_width)
    )
    first_part = jnp.dot(by_virtual, by_virtual.T, preferred_element_type=jnp.float32)
    by_column = amp_half.reshape(row_count * occ_width, vir_width)
    second_part = jnp.dot(by_column.T, by_column, preferred_element_type=jnp.float32)
    collected = first_part
    for distance in range(1, REACH + 1):
        outgoing = jnp.where(partner_step == distance, second_part, jnp.float32(0.0))
        collected = collected + passed_along(outgoing, "frag", distance)
    density = lax.psum_scatter(collected, "aux", scatter_dimension=0, tiled=True)
    return (energy.reshape(1), density[None])


def solution(mesh):
    placed = (P("frag", "aux", None), P(), P(), P(), P(), P("frag"))
    return jax.shard_map(
        on_device,
        mesh=mesh,
        in_specs=placed,
        out_specs=(P("frag"), P("frag", "aux", None)),
        check_vma=False,
    )
```

profile of v0, /device:TPU:1, one launch (start us, length us, event | category | flops | bytes accessed | tf_op | source)
XLA Modules:
  0.0 786.2 jit_solution(2633305769924106858)
XLA Ops:
  7.2 3.3 collective-permute-start
  10.6 1.3 collective-permute-start.1
  11.9 1.3 collective-permute-start.2
  13.8 196.1 %collective-permute-done = bf16[1,752,4096]{2,1,0:T(8,128)(2,1)} collective-permute-done((bf16[1,752,4096]{2,1,0:T(8,128)(2,1)}, bf16[1,752,4096]{2,1,0:T(8,128)(2,1)}, u32[]{:S(2)}, u32[]{:S(2)}) %collective-permute-start) | collective-permute-done | bytes 6160416 | tf_op jit(solution)/shard_map/ppermute | solution.py:12
  209.9 3.9 collective-permute-done.1
  213.8 8.3 %fusion.7 = bf16[1,752,4096]{2,1,0:T(8,128)(2,1)} fusion(s32[]{:T(128)S(6)} %select_n.49, bf16[1,752,4096]{2,1,0:T(8,128)(2,1)} %param.6, bf16[1,752,4096]{2,1,0:T(8,128)(2,1)} %collective-permute-done, bf16[1,752,4096]{2,1,0:T(8,128)(2,1)} %collective-permute-done.1, bf16[1,752,4096]{2,1,0:T(8,128)(2,1)} %collective-permute-done.2), kind=kLoop, calls=%fused_computation.13 | loop fusion | flops 9240576 | bytes 30801924 | tf_op jit(solution)/shard_map/concatenate | solution.py:32
  222.2 8.5 %copy.10 = bf16[1,752,4096]{1,2,0:T(8,128)(2,1)} copy(bf16[1,752,4096]{2,1,0:T(8,128)(2,1)} %param.6) | data formatting | bytes 12320768 | tf_op args[0]
  230.7 8.7 %copy.11 = bf16[752,4,1024]{2,0,1:T(8,128)(2,1)} copy(bf16[752,4,1024]{0,2,1:T(8,128)(2,1)} %bitcast.58) | data formatting | bytes 12320768 | tf_op jit(solution)/shard_map/all_to_all | solution.py:34
  239.3 5.4 all-to-all-start
  244.7 0.2 reduce-scatter.2.cloned.1.call-start
  245.0 0.7 fusion.11
  245.6 0.7 add_compare_fusion
  246.3 0.6 iota_compare_fusion.1
  247.0 0.6 iota_compare_fusion
  247.7 0.6 iota_compare_fusion.2
  248.2 0.1 broadcast_and_fusion
  248.3 0.2 dynamic-slice_reduce_fusion
  248.5 0.8 constant_dynamic-slice_fusion.1
  249.4 0.2 dynamic-slice_reduce_fusion.1
  249.7 32.2 %all-to-all-done = bf16[752,4,1024]{2,0,1:T(8,128)(2,1)} async-done(((bf16[752,4,1024]{2,0,1:T(8,128)(2,1)}), bf16[752,4,1024]{2,0,1:T(8,128)(2,1)}, u32[]{:S(2)}, u32[]{:S(2)}) %all-to-all-start) | async-done | bytes 6160416 | tf_op jit(solution)/shard_map/all_to_all | solution.py:34
  281.9 359.6 %all-gather.3.cloned.1.call-done = bf16[1,3008,4096]{2,1,0:T(8,128)(2,1)} async-done(((bf16[1,752,4096]{2,1,0:T(8,128)(2,1)}), bf16[1,3008,4096]{2,1,0:T(8,128)(2,1)}) %all-gather.3.cloned.1.call-update) | async-done | bytes 24641552 | tf_op jit(solution)/shard_map/all_gather | solution.py:37
  641.5 39.2 %fusion.4 = (bf16[1024,4096]{1,0:T(8,128)(2,1)}, f32[]{:T(128)}) fusion(f32[4096]{0:T(1024)S(1)} %bitcast.60, f32[1024]{0:T(1024)S(1)} %bitcast.62, pred[]{:T(512)S(6)} %lt.72, pred[4096]{0:T(1024)(128)(4,1)S(1)} %and.69, pred[1024]{0:T(1024)(128)(4,1)S(1)} %and.64, bf16[3008,1024]{1,0:T(8,128)(2,1)} %bitcast.8, ...), kind=kOutput, calls=%fused_computation.10 | convolution fusion | flops 25266487296 | bytes 39216132 | tf_op jit(solution)/shard_map/dot_general | solution.py:35
  680.7 13.5 %reshape.97 = bf16[16384,256]{1,0:T(8,128)(2,1)} reshape(bf16[1024,4096]{1,0:T(8,128)(2,1)} %get-tuple-element.2) | data formatting | bytes 16777216 | tf_op jit(solution)/shard_map/reshape | solution.py:67
  694.2 8.3 %broadcast_select_fusion.2 = (f32[256,256]{1,0:T(8,128)S(1)}, f32[256,256]{1,0:T(8,128)S(1)}, f32[256,256]{1,0:T(8,128)S(1)}) fusion(pred[]{:T(512)S(6)} %eq.9, pred[]{:T(512)S(6)} %eq.11, pred[]{:T(512)S(6)} %eq.10, bf16[16384,256]{1,0:T(8,128)(2,1)} %reshape.97), kind=kOutput, calls=%fused_computation.20 | convolution fusion | flops 2147680256 | bytes 9175043 | tf_op jit(solution)/shard_map/dot_general | solution.py:68
  702.5 3.8 collective-permute-start.3
  706.3 36.2 %collective-permute-start.4 = (f32[256,256]{1,0:T(8,128)S(1)}, f32[256,256]{1,0:T(8,128)S(1)}, u32[]{:S(2)}, u32[]{:S(2)}) collective-permute-start(f32[256,256]{1,0:T(8,128)S(1)} %get-tuple-element.6), channel_id=1, source_target_pairs={{0,8},{4,12},{8,16},{12,20},{16,24},{20,28},{24,32},{28,36},{32,40... | collective-permute-start | bytes 786440 | tf_op jit(solution)/shard_map/ppermute | solution.py:12
  742.5 2.3 collective-permute-start.5
  744.7 1.2 collective-permute-done.4
  746.0 5.4 collective-permute-done.5
  751.4 3.1 fusion.10
  754.4 7.9 %psum.7 = f32[1]{0:T(128)} all-reduce(f32[1]{0:T(128)} %bitcast.12), channel_id=1, replica_groups=mesh['frag'=32,'aux'=4] {'aux'}, use_global_device_ids=true, to_apply=%region_1.2 | all-reduce | flops 1 | bytes 8 | tf_op jit(solution)/shard_map/psum | solution.py:59
  762.4 17.0 %reduce-scatter.2.cloned.1.call-done = f32[64,256]{1,0:T(8,128)} async-done(((f32[256,256]{1,0:T(8,128)}), f32[64,256]{1,0:T(8,128)}) %reduce-scatter.2.cloned.1.call-update) | async-done | bytes 65552 | tf_op jit(solution)/shard_map/reduce_scatter | solution.py:73
  (22 shorter events, 0.4 us)
Async XLA Ops:
  7.2 241.1 %copy-start = (f32[32,16]{0,1:T(8,128)S(1)}, f32[32,16]{0,1:T(8,128)}, u32[]{:S(2)}) copy-start(f32[32,16]{0,1:T(8,128)} %param.7) | copy-start | bytes 6148
  7.2 634.3 %all-gather.3.cloned.1.call-start = ((), (), s32[]{:S(2)}) async-start(), calls=%async_computation.3 | async-start | bytes 30801920 | tf_op jit(solution)/shard_map/all_gather | solution.py:37
  7.2 202.7 %collective-permute-start = (bf16[1,752,4096]{2,1,0:T(8,128)(2,1)}, bf16[1,752,4096]{2,1,0:T(8,128)(2,1)}, u32[]{:S(2)}, u32[]{:S(2)}) collective-permute-start(bf16[1,752,4096]{2,1,0:T(8,128)(2,1)} %param.6), channel_id=1, source_target_pairs={{4,0},{8,4},{12,8},{16,12},{20,16},{24,20},{28,24},{32,28},{36,32}... | collective-permute-start | bytes 18481160 | tf_op jit(solution)/shard_map/ppermute | solution.py:12
  10.6 203.3 %collective-permute-start.1 = (bf16[1,752,4096]{2,1,0:T(8,128)(2,1)}, bf16[1,752,4096]{2,1,0:T(8,128)(2,1)}, u32[]{:S(2)}, u32[]{:S(2)}) collective-permute-start(bf16[1,752,4096]{2,1,0:T(8,128)(2,1)} %param.6), channel_id=1, source_target_pairs={{8,0},{12,4},{16,8},{20,12},{24,16},{28,20},{32,24},{36,28},{40,32... | collective-permute-start | bytes 18481160 | tf_op jit(solution)/shard_map/ppermute | solution.py:12
  11.9 202.0 %collective-permute-start.2 = (bf16[1,752,4096]{2,1,0:T(8,128)(2,1)}, bf16[1,752,4096]{2,1,0:T(8,128)(2,1)}, u32[]{:S(2)}, u32[]{:S(2)}) collective-permute-start(bf16[1,752,4096]{2,1,0:T(8,128)(2,1)} %param.6), channel_id=1, source_target_pairs={{12,0},{16,4},{20,8},{24,12},{28,16},{32,20},{36,24},{40,28},{44,3... | collective-permute-start | bytes 18481160 | tf_op jit(solution)/shard_map/ppermute | solution.py:12
  239.3 5.6 copy-start.3
  239.3 5.6 copy-start.4
  239.3 42.6 %all-to-all-start = ((bf16[752,4,1024]{2,0,1:T(8,128)(2,1)}), bf16[752,4,1024]{2,0,1:T(8,128)(2,1)}, u32[]{:S(2)}, u32[]{:S(2)}) async-start(bf16[752,4,1024]{2,0,1:T(8,128)(2,1)} %copy.11), calls=%async_computation | async-start | bytes 12320768 | tf_op jit(solution)/shard_map/all_to_all | solution.py:34
  244.7 534.7 %reduce-scatter.2.cloned.1.call-start = ((), (), s32[]{:S(2)}) async-start(), calls=%async_computation.2 | async-start | bytes 327680 | tf_op jit(solution)/shard_map/reduce_scatter | solution.py:73
  694.2 57.1 %copy-start.2 = (bf16[1024,4096]{1,0:T(8,128)(2,1)S(1)}, bf16[1024,4096]{1,0:T(8,128)(2,1)}, u32[]{:S(2)}) copy-start(bf16[1024,4096]{1,0:T(8,128)(2,1)} %get-tuple-element.2) | copy-start | bytes 25165828
  702.5 42.2 %collective-permute-start.3 = (f32[256,256]{1,0:T(8,128)S(1)}, f32[256,256]{1,0:T(8,128)S(1)}, u32[]{:S(2)}, u32[]{:S(2)}) collective-permute-start(f32[256,256]{1,0:T(8,128)S(1)} %get-tuple-element.4), channel_id=1, source_target_pairs={{0,4},{4,8},{8,12},{12,16},{16,20},{20,24},{24,28},{28,32},{32,36}... | collective-permute-start | bytes 786440 | tf_op jit(solution)/shard_map/ppermute | solution.py:12
  706.3 39.7 %collective-permute-start.4 = (f32[256,256]{1,0:T(8,128)S(1)}, f32[256,256]{1,0:T(8,128)S(1)}, u32[]{:S(2)}, u32[]{:S(2)}) collective-permute-start(f32[256,256]{1,0:T(8,128)S(1)} %get-tuple-element.6), channel_id=1, source_target_pairs={{0,8},{4,12},{8,16},{12,20},{16,24},{20,28},{24,32},{28,36},{32,40... | collective-permute-start | bytes 786440 | tf_op jit(solution)/shard_map/ppermute | solution.py:12
  742.5 8.9 %collective-permute-start.5 = (f32[256,256]{1,0:T(8,128)S(1)}, f32[256,256]{1,0:T(8,128)S(1)}, u32[]{:S(2)}, u32[]{:S(2)}) collective-permute-start(f32[256,256]{1,0:T(8,128)S(1)} %get-tuple-element.5), channel_id=1, source_target_pairs={{0,12},{4,16},{8,20},{12,24},{16,28},{20,32},{24,36},{28,40},{32,4... | collective-permute-start | bytes 786440 | tf_op jit(solution)/shard_map/ppermute | solution.py:12
  751.4 28.0 %copy-start.1 = (f32[32,16]{0,1:T(8,128)S(1)}, f32[32,16]{0,1:T(8,128)}, u32[]{:S(2)}) copy-start(f32[32,16]{0,1:T(8,128)} %param.7) | copy-start | bytes 6148
Sparse Core Ops, SparseCore 0:
  222.3 419.1 all-gather.2
  754.6 24.7 reduce-scatter.1
where the time goes:
time: 789 us; the launch traced here: 786 us
  waiting for transfers between devices  616 us (78%)
  starting transfers between devices  53.7 us (7%)
  matrix products  50.6 us (6%)
  local copies, waits for them, and re-layouts  32.5 us (4%)
  between operations  14.9 us (2%)
  other arithmetic  11.1 us (1%)
  blocking collectives  7.93 us (1%)
    all_gather x1, waiting for transfers between devices, on_device(): lax.all_gather(partner_block, 'aux', axis=0, tiled=True)  360 us
    ppermute x6, waiting for transfers between devices, passed_along(): return lax.ppermute(array, axis, pairs)  207 us
    ppermute x6, starting transfers between devices, passed_along(): return lax.ppermute(array, axis, pairs)  48.1 us
    dot_general x1, matrix products, on_device(): lax.dot_general(own_rows, lax.all_gather(partner_block, 'aux', axis=0, ti...  39.2 us
    all_to_all x1, waiting for transfers between devices, on_device(): lax.all_to_all(own_block, 'aux', split_axis=1, concat_axis=0, tiled=True)  32.2 us
    reduce_scatter x1, waiting for transfers between devices, on_device(): lax.psum_scatter(collected, 'aux', scatter_dimension=0, tiled=True)  17 us
  transfers between devices with their start and end apart: 9, of which 7 were waited for; matrix products, arithmetic and copies ran while one was open for 3% of the time, Pallas kernels for 0%

commit v1 on v0

v1 whole, which is shorter than its diff:
```python
import functools

import jax
import jax.numpy as jnp
from jax import lax
from jax.experimental import pallas as pl
from jax.experimental.pallas import tpu as pltpu
from jax.sharding import PartitionSpec as P

LEAD = 2
PIECES = 4
BLOCK = 256


def pieces_of(rows):
    step = -(-rows // (16 * PIECES)) * 16
    return [(at, min(step, rows - at)) for at in range(0, rows, step)]


def to_device(src, dst, send_sem, recv_sem, frag, aux):
    return pltpu.make_async_remote_copy(
        src_ref=src,
        dst_ref=dst,
        send_sem=send_sem,
        recv_sem=recv_sem,
        device_id={"frag": frag, "aux": aux},
        device_id_type=pl.DeviceIdType.MESH,
    )


def kernel(
    frag_total,
    blocks,
    occ_energy,
    vir_energy,
    occ_count,
    vir_count,
    offset,
    energy_out,
    density_out,
    a_half,
    a_other,
    b_half,
    b_other,
    cand,
    b_turned,
    base,
    keep,
    total,
    landed,
    summed,
    parts,
    off_send,
    off_here,
    off_scalar,
    a_in,
    a_up,
    a_send,
    a_recv,
    cand_send,
    cand_recv,
    cand_pass,
    b_send,
    b_recv,
    off_sems,
    sum_send,
    sum_recv,
    part_send,
    part_recv,
):
    rows = blocks.shape[1]
    half = blocks.shape[2] // 2
    vir = vir_energy.shape[1]
    steps = b_half.shape[0]
    pieces = pieces_of(rows)
    padded = a_half.shape[0]
    aux_rows = vir // 4
    chips = frag_total // 2

    frag = lax.axis_index("frag")
    aux = lax.axis_index("aux")
    core = lax.rem(frag, 2)
    chip = frag // 2
    up = lax.rem(chip + 1, chips)
    down = lax.rem(chip + chips - 1, chips)
    sibling = chip * 2 + 1 - core

    near = aux + 1 - 2 * lax.rem(aux, 2)
    side = 3 - aux
    far = lax.rem(aux + 2, 4)
    by_near = aux // 2
    by_side = lax.rem((aux + 1) // 2, 2)
    a_mate = jnp.where(core == 0, near, side)
    b_mate = jnp.where(core == 0, side, near)
    p_half = jnp.where(core == 0, by_near, by_side)
    q_half = jnp.where(core == 0, by_side, by_near)

    barrier = pltpu.get_barrier_semaphore()
    for other in (near, side, far):
        pl.semaphore_signal(
            barrier, inc=1, device_id={"frag": frag, "aux": other}, device_id_type=pl.DeviceIdType.MESH
        )
    for other in (sibling, up * 2, up * 2 + 1, down * 2, down * 2 + 1):
        pl.semaphore_signal(
            barrier, inc=1, device_id={"frag": other, "aux": aux}, device_id_type=pl.DeviceIdType.MESH
        )
    pl.semaphore_wait(barrier, 8)

    p_cols = pl.ds(pl.multiple_of(p_half * half, 256), half)
    p_rest = pl.ds(pl.multiple_of((1 - p_half) * half, 256), half)

    def own_rows(who, at, size):
        return pl.ds(pl.multiple_of(who * rows + at, 16), size)

    def a_first(n, at, size, there):
        src = blocks.at[0, pl.ds(at, size), p_cols]
        dst = a_half.at[own_rows(aux, at, size)]
        if there is None:
            return pltpu.make_async_copy(src, dst, a_in.at[0, n])
        return to_device(src, dst, a_up.at[0, n], a_in.at[0, n], there, aux)

    def a_second(n, at, size, there):
        src = blocks.at[0, pl.ds(at, size), p_rest]
        dst = a_other.at[pl.ds(at, size)]
        if there is None:
            return pltpu.make_async_copy(src, dst, a_in.at[1, n])
        return to_device(src, dst, a_up.at[1, n], a_in.at[1, n], there, aux)

    def off_copy():
        return to_device(off_send, off_here, off_sems.at[0], off_sems.at[1], up * 2 + 1, aux)

    def cand_copy(j, slot, n, there):
        src = blocks.at[0, :, pl.ds(pl.multiple_of(j * 2 * vir, 256), 2 * vir)]
        if there is None:
            return pltpu.make_async_copy(src, cand.at[slot, j], cand_recv.at[slot, j])
        return to_device(src, cand.at[slot, j], cand_send.at[n, j], cand_recv.at[slot, j], there, aux)

    def cand_forward(j):
        return to_device(cand.at[2, j], cand.at[1, j], cand_pass.at[j], cand_recv.at[1, j], sibling, aux)

    off_send[...] = jnp.full(off_send.shape, offset[0], jnp.int32)

    @pl.when(core == 0)
    def _():
        for n, (at, size) in enumerate(pieces):
            a_first(n, at, size, None).start()
            a_second(n, at, size, None).start()

        @pl.loop(0, steps)
        def _(j):
            cand_copy(j, 2, 1, down * 2 + 1).start()
            cand_copy(j, 0, 0, sibling).start()

    @pl.when(core == 1)
    def _():
        off_copy().start()
        for n, (at, size) in enumerate(pieces):
            a_first(n, at, size, up * 2 + 1).start()
            a_second(n, at, size, up * 2 + 1).start()

        @pl.loop(0, steps)
        def _(j):
            cand_copy(j, 2, 1, down * 2).start()
            cand_copy(j, 0, 0, sibling).start()
            cand_copy(j, 1, 0, None).start()

    def a_direct(n, at, size):
        here = a_half.at[own_rows(aux, at, size)]
        return to_device(here, here, a_send.at[0, n], a_recv.at[0, n], frag, a_mate)

    def a_across(n, at, size):
        return to_device(
            a_other.at[pl.ds(at, size)],
            a_half.at[own_rows(aux, at, size)],
            a_send.at[1, n],
            a_recv.at[1, n],
            frag,
            b_mate,
        )

    def a_forward(n, at, size):
        here = a_half.at[own_rows(b_mate, at, size)]
        return to_device(here, here, a_send.at[2, n], a_recv.at[2, n], frag, a_mate)

    def a_landing(kind, who, n, at, size):
        here = a_half.at[own_rows(who, at, size)]
        return to_device(here, here, a_send.at[kind, n], a_recv.at[kind, n], frag, a_mate)

    if padded > 4 * rows:
        a_half[4 * rows :, :] = jnp.zeros((padded - 4 * rows, half), jnp.bfloat16)

        @pl.loop(0, steps)
        def _(j):
            b_half[j, 4 * rows :, :] = jnp.zeros((padded - 4 * rows, vir), jnp.bfloat16)

    for n, (at, size) in enumerate(pieces):
        @pl.when(core == 0)
        def _():
            a_first(n, at, size, None).wait()
            a_second(n, at, size, None).wait()

        @pl.when(core == 1)
        def _():
            a_first(n, at, size, up * 2 + 1).wait_recv()
            a_second(n, at, size, up * 2 + 1).wait_recv()

        a_across(n, at, size).start()
        a_direct(n, at, size).start()

    @pl.when(core == 0)
    def _():
        off_here[...] = off_send[...]

    @pl.when(core == 1)
    def _():
        off_copy().wait()

    scalar_copy = pltpu.make_async_copy(off_here, off_scalar, off_sems.at[2])
    scalar_copy.start()
    scalar_copy.wait()
    distance = off_scalar[0, 0]
    leader = jnp.where(core == 0, frag, lax.rem(chip * 2 + frag_total - 1, frag_total))
    partner = jnp.minimum(leader + distance, frag_total - 1)
    valid = leader + distance < frag_total
    leader_occ = occ_count[leader]
    partner_occ = occ_count[partner]
    leader_vir = vir_count[leader]
    partner_vir = vir_count[partner]

    row_levels = jnp.broadcast_to(vir_energy[pl.ds(partner, 1), :], (vir, vir)).T
    base[...] = -vir_energy[pl.ds(leader, 1), :] - row_levels
    row_ids = lax.broadcasted_iota(jnp.int32, (vir, vir), 0)
    col_ids = lax.broadcasted_iota(jnp.int32, (vir, vir), 1)
    keep[...] = jnp.where((row_ids < partner_vir) & (col_ids < leader_vir), 1.0, 0.0)
    total[...] = jnp.zeros(total.shape, jnp.float32)

    for n, (at, size) in enumerate(pieces):
        a_landing(1, b_mate, n, at, size).wait_recv()
        a_forward(n, at, size).start()

    def b_direct(j):
        here = b_half.at[j, own_rows(aux, 0, rows)]
        return to_device(here, here, b_send.at[0, j], b_recv.at[0, j], frag, b_mate)

    def b_across(j):
        return to_device(
            b_other.at[j],
            b_half.at[j, own_rows(aux, 0, rows)],
            b_send.at[1, j],
            b_recv.at[1, j],
            frag,
            a_mate,
        )

    def b_forward(j):
        here = b_half.at[j, own_rows(a_mate, 0, rows)]
        return to_device(here, here, b_send.at[2, j], b_recv.at[2, j], frag, b_mate)

    def b_landing(kind, who, j):
        here = b_half.at[j, own_rows(who, 0, rows)]
        return to_device(here, here, b_send.at[kind, j], b_recv.at[kind, j], frag, b_mate)

    def chosen(j, which):
        cols = pl.ds(pl.multiple_of(which * vir, 128), vir)
        one, two, three = (cand[n, j, :, cols] for n in range(3))
        return jnp.where(distance == 1, one, jnp.where(distance == 2, two, three))

    def begin(j):
        @pl.when(core == 1)
        def _():
            cand_copy(j, 2, 1, down * 2).wait_recv()
            cand_forward(j).start()
            cand_copy(j, 0, 0, sibling).wait_recv()
            cand_copy(j, 1, 0, None).wait()

        @pl.when(core == 0)
        def _():
            cand_copy(j, 0, 0, sibling).wait_recv()
            cand_copy(j, 2, 1, down * 2).wait_recv()
            cand_forward(j).wait_recv()

        b_other[j] = chosen(j, 1 - q_half)
        b_across(j).start()
        b_half[j, own_rows(aux, 0, rows), :] = chosen(j, q_half)
        b_direct(j).start()

    def pass_on(j):
        b_landing(1, a_mate, j).wait_recv()
        b_forward(j).start()

    def work(j):
        for at in range(0, padded, BLOCK):
            b_turned[:, at : at + BLOCK] = b_half[j, at : at + BLOCK, :].T
        col_occ = 2 * j + q_half
        col_level = occ_energy[partner, col_occ]
        col_ok = jnp.logical_and(valid, col_occ < partner_occ)

        def tile(i, carry):
            row_occ = p_half * steps + i
            ok = jnp.where(jnp.logical_and(col_ok, row_occ < leader_occ), 1.0, 0.0)
            level = occ_energy[leader, row_occ] + col_level
            integrals = jnp.dot(
                b_turned[...],
                a_half[:, pl.ds(pl.multiple_of(i * vir, 128), vir)],
                preferred_element_type=jnp.float32,
            )
            amplitude = integrals * (keep[...] * ok) / (base[...] + level)
            energy = amplitude * integrals
            rounded = amplitude.astype(jnp.bfloat16)
            first = lax.dot_general(
                rounded, rounded, (((0,), (0,)), ((), ())), preferred_element_type=jnp.float32
            )
            second = lax.dot_general(
                rounded, rounded, (((1,), (1,)), ((), ())), preferred_element_type=jnp.float32
            )
            for n in range(4):
                piece = slice(n * aux_rows, (n + 1) * aux_rows)
                total[n, :aux_rows, :] += first[piece]
                total[n, aux_rows : 2 * aux_rows, :] += second[piece]
            total[0, 2 * aux_rows :, :] += energy.reshape(vir // 8, 8, vir).sum(0)
            return carry

        lax.fori_loop(0, steps, tile, 0)

    for j in range(LEAD):
        begin(j)
    pass_on(0)

    for n, (at, size) in enumerate(pieces):
        a_landing(0, a_mate, n, at, size).wait_recv()
        a_landing(2, far, n, at, size).wait_recv()

    @pl.loop(0, steps)
    def _(j):
        @pl.when(j + LEAD < steps)
        def _():
            begin(j + LEAD)

        @pl.when(j + 1 < steps)
        def _():
            pass_on(j + 1)

        b_landing(0, b_mate, j).wait_recv()
        b_landing(2, far, j).wait_recv()
        work(j)

    for n in range(1, 4):
        total[n, 2 * aux_rows :, :] = total[0, 2 * aux_rows :, :]

    def sum_copy(n):
        there = lax.rem(aux + n, 4)
        return to_device(
            total.at[there], landed.at[4 - n], sum_send.at[n - 1], sum_recv.at[n - 1], frag, there
        )

    for n in (2, 1, 3):
        sum_copy(n).start()
    landed[0] = total[aux]
    for n in (1, 3, 2):
        sum_copy(n).wait()
    sums = landed[lax.rem(4 - aux, 4)]
    for n in range(1, 4):
        sums = sums + landed[lax.rem(n + 4 - aux, 4)]
    summed[0, :aux_rows, :] = sums[:aux_rows]
    summed[0, aux_rows:, :] = sums[2 * aux_rows :]
    for n in range(1, 4):
        summed[n, :aux_rows, :] = jnp.where(distance == n, sums[aux_rows : 2 * aux_rows], 0.0)

    def part_copy(n, there):
        if n == 0:
            src, dst = summed.at[0], parts.at[0]
        else:
            src, dst = summed.at[n, pl.ds(0, aux_rows)], parts.at[n, pl.ds(0, aux_rows)]
        return to_device(src, dst, part_send.at[n], part_recv.at[n], there, aux)

    @pl.when(core == 0)
    def _():
        part_copy(3, up * 2 + 1).start()
        part_copy(2, up * 2).start()
        part_copy(1, sibling).start()
        parts[0] = summed[0]
        for n in (1, 2, 3):
            part_copy(n, sibling).wait()

    @pl.when(core == 1)
    def _():
        part_copy(0, down * 2 + 1).start()
        part_copy(3, up * 2).start()
        part_copy(1, sibling).start()
        parts[2, :aux_rows, :] = summed[2, :aux_rows, :]
        for n in (1, 3, 0):
            part_copy(n, sibling).wait()

    density_out[0] = (
        parts[0, :aux_rows, :] + parts[1, :aux_rows, :] + parts[2, :aux_rows, :] + parts[3, :aux_rows, :]
    )
    energy_out[0] = jnp.sum(parts[0, aux_rows:, :])

    @pl.when(core == 1)
    def _():
        for n, (at, size) in enumerate(pieces):
            a_first(n, at, size, up * 2 + 1).wait_send()
            a_second(n, at, size, up * 2 + 1).wait_send()

        @pl.loop(0, steps)
        def _(j):
            cand_forward(j).wait_send()

    for n, (at, size) in enumerate(pieces):
        a_direct(n, at, size).wait_send()
        a_across(n, at, size).wait_send()
        a_forward(n, at, size).wait_send()

    @pl.loop(0, steps)
    def _(j):
        cand_copy(j, 0, 0, sibling).wait_send()
        cand_copy(j, 2, 1, sibling).wait_send()
        b_direct(j).wait_send()
        b_across(j).wait_send()
        b_forward(j).wait_send()


def on_device(blocks, occ_energy, vir_energy, occ_count, vir_count, partner_offset):
    frag_total, occ = occ_energy.shape
    vir = vir_energy.shape[1]
    rows = blocks.shape[1]
    half = occ * vir // 2
    steps = occ // 2
    padded = -(-4 * rows // BLOCK) * BLOCK
    aux_rows = vir // 4
    n_pieces = len(pieces_of(rows))
    vmem = pl.BlockSpec(memory_space=pltpu.VMEM)
    smem = pl.BlockSpec(memory_space=pltpu.SMEM)
    dma = pltpu.SemaphoreType.DMA
    return pl.pallas_call(
        functools.partial(kernel, frag_total),
        out_shape=(
            jax.ShapeDtypeStruct((1,), jnp.float32),
            jax.ShapeDtypeStruct((1, aux_rows, vir), jnp.float32),
        ),
        in_specs=[pl.BlockSpec(memory_space=pl.ANY), smem, vmem, smem, smem, smem],
        out_specs=(smem, vmem),
        scratch_shapes=[
            pltpu.VMEM((padded, half), jnp.bfloat16),
            pltpu.VMEM((rows, half), jnp.bfloat16),
            pltpu.VMEM((steps, padded, vir), jnp.bfloat16),
            pltpu.VMEM((steps, rows, vir), jnp.bfloat16),
            pltpu.VMEM((3, steps, rows, 2 * vir), jnp.bfloat16),
            pltpu.VMEM((vir, padded), jnp.bfloat16),
            pltpu.VMEM((vir, vir), jnp.float32),
            pltpu.VMEM((vir, vir), jnp.float32),
            pltpu.VMEM((4, 2 * aux_rows + 8, vir), jnp.float32),
            pltpu.VMEM((4, 2 * aux_rows + 8, vir), jnp.float32),
            pltpu.VMEM((4, aux_rows + 8, vir), jnp.float32),
            pltpu.VMEM((4, aux_rows + 8, vir), jnp.float32),
            pltpu.VMEM((8, 128), jnp.int32),
            pltpu.VMEM((8, 128), jnp.int32),
            pltpu.SMEM((8, 128), jnp.int32),
            dma((2, n_pieces)),
            dma((2, n_pieces)),
            dma((3, n_pieces)),
            dma((3, n_pieces)),
            dma((2, steps)),
            dma((3, steps)),
            dma((steps,)),
            dma((3, steps)),
            dma((3, steps)),
            dma((3,)),
            dma((3,)),
            dma((3,)),
            dma((4,)),
            dma((4,)),
        ],
        compiler_params=pltpu.CompilerParams(
            collective_id=0, has_side_effects=True, vmem_limit_bytes=60 * 1024 * 1024
        ),
        cost_estimate=pl.CostEstimate(
            flops=2 * 4 * rows * half * half, bytes_accessed=2 * rows * 2 * half, transcendentals=0
        ),
        name="pair_terms",
    )(blocks, occ_energy, vir_energy, occ_count, vir_count, partner_offset)


def solution(mesh):
    placed = (P("frag", "aux", None), P(), P(), P(), P(), P("frag"))
    return jax.shard_map(
        on_device,
        mesh=mesh,
        in_specs=placed,
        out_specs=(P("frag"), P("frag", "aux", None)),
        check_vma=False,
    )
```

time: 789 us -> 254 us (0.32)
  waiting for transfers between devices: 616 us -> 0 us
  Pallas kernels: 0 us -> 248 us
  starting transfers between devices: 53.7 us -> 0 us
  matrix products: 50.6 us -> 0 us
  local copies, waits for them, and re-layouts: 32.5 us -> 2.85 us
  between operations: 14.9 us -> 3.03 us
  other arithmetic: 11.1 us -> 0 us
  blocking collectives: 7.93 us -> 0 us
    all_gather x1 -> x0, waiting for transfers between devices: 360 us -> none  [on_device(): lax.all_gather(partner_block, 'aux', axis=0, tiled=True)]
    pallas_call x0 -> x1, Pallas kernels: none -> 248 us  [on_device(): pl.pallas_call(functools.partial(kernel, frag_total), out_shape=(jax.Shap...]
    ppermute x6 -> x0, waiting for transfers between devices: 207 us -> none  [passed_along(): return lax.ppermute(array, axis, pairs)]
    dot_general x3 -> x0, matrix products: 50.6 us -> none  [the longest x1 39.2 us: on_device(): lax.dot_general(own_rows, lax.all_gather(partner_block, 'aux', axis=0, ti...]
    ppermute x6 -> x0, starting transfers between devices: 48.1 us -> none  [passed_along(): return lax.ppermute(array, axis, pairs)]
    all_to_all x1 -> x0, waiting for transfers between devices: 32.2 us -> none  [on_device(): lax.all_to_all(own_block, 'aux', split_axis=1, concat_axis=0, tiled=True)]
    reduce_scatter x1 -> x0, waiting for transfers between devices: 17 us -> none  [on_device(): lax.psum_scatter(collected, 'aux', scatter_dimension=0, tiled=True)]
    reshape x1 -> x0, local copies, waits for them, and re-layouts: 13.5 us -> none  [on_device(): by_column = amp_half.reshape(row_count * occ_width, vir_width)]
  transfers between devices with their start and end apart: 9 -> 0, of which waited for: 7 -> 0; matrix products, arithmetic and copies ran while one was open for 3% -> 0% of each run, Pallas kernels for 0% -> 0%
where the time goes in v1:
time: 254 us; the launch traced here: 253 us
  Pallas kernels  248 us (98%)
  between operations  3.03 us (1%)
  local copies, waits for them, and re-layouts  2.85 us (1%)
    pallas_call x1, Pallas kernels, on_device(): pl.pallas_call(functools.partial(kernel, frag_total), out_shape=(jax.Shap...  248 us

profile of v1, /device:TPU:1, one launch (start us, length us, event | category | flops | bytes accessed | tf_op | source)
XLA Modules:
  0.0 253.4 jit_solution(13396480226091999402)
XLA Ops:
  1.3 1.4 copy.8.occ_energy
  2.7 247.6 %pair_terms.1 = (f32[1]{0:T(128)}, f32[1,64,256]{2,1,0:T(8,128)}) custom-call(bf16[1,752,4096]{2,1,0:T(8,128)(2,1)} %blocks.1, f32[32,16]{1,0:T(8,128)} %copy.8.occ_energy, f32[32,256]{1,0:T(8,128)} %vir_energy.1, s32[32]{0:T(128)} %occ_count.1, s32[32]{0:T(128)} %vir_count.1, s32[1]{0:T(128)S(6)} %copy.11.offset), custom_call_target="tpu_custom_call" | custom-call | flops 25232932864 | bytes 6160384 | tf_op jit(solution)/shard_map/pair_terms/pallas_call | solution.py:435
  250.8 1.5 copy.13

commit v2 on v0

v2 whole, which is shorter than its diff:
```python
import functools

import jax
import jax.numpy as jnp
from jax import lax
from jax.experimental import pallas as pl
from jax.experimental.pallas import tpu as pltpu
from jax.sharding import PartitionSpec as P

LEAD = 2
BLOCK = 256
ROW_FRAGS = 8
MESH = pl.DeviceIdType.MESH


def to_device(src, dst, send_sem, recv_sem, frag, aux):
    return pltpu.make_async_remote_copy(
        src_ref=src,
        dst_ref=dst,
        send_sem=send_sem,
        recv_sem=recv_sem,
        device_id={"frag": frag, "aux": aux},
        device_id_type=MESH,
    )


def place_in_ring(aux, row):
    turn = lax.rem(row, 2)
    at = lax.rem(aux + 4 - turn, 4)
    mate = lax.rem(at + 1 - 2 * lax.rem(at, 2) + turn, 4)
    outer = lax.rem(3 - at + turn, 4)
    return at // 2, lax.rem(at, 2), mate, outer


def kernel(
    frag_total,
    blocks,
    occ_energy_in,
    vir_energy_in,
    occ_count_in,
    vir_count_in,
    offset_in,
    energy_out,
    density_out,
    a_stage,
    transit,
    relay,
    occ_energy,
    vir_energy,
    occ_count,
    vir_count,
    offset,
    a_half,
    b_half,
    b_other,
    b_mine,
    cand,
    a_turned,
    b_turned,
    base,
    keep,
    total,
    landed,
    summed,
    parts,
    off_vectors,
    off_scalars,
    in_sems,
    z_send,
    z_recv,
    a_send,
    a_recv,
    cand_send,
    cand_recv,
    cand_pass,
    b_send,
    b_recv,
    b_share,
    relay_recv,
    off_sems,
    sum_send,
    sum_recv,
    part_send,
    part_recv,
):
    rows = blocks.shape[1]
    steps, padded, vir = a_half.shape
    aux_rows = vir // 4
    chips = frag_total // 2
    grid_rows = frag_total // ROW_FRAGS

    frag = lax.axis_index("frag")
    aux = lax.axis_index("aux")
    core = lax.rem(frag, 2)
    chip = frag // 2
    row = frag // ROW_FRAGS
    up = lax.rem(chip + 1, chips)
    down = lax.rem(chip + chips - 1, chips)
    sibling = chip * 2 + 1 - core
    next_row = lax.rem(frag + ROW_FRAGS, frag_total)
    last_row = lax.rem(frag + frag_total - ROW_FRAGS, frag_total)

    pair, q_half, mate, outer = place_in_ring(aux, row)
    far = lax.rem(aux + 2, 4)
    member = core == pair
    stranger = core != pair
    relay_pair, _, relay_to, _ = place_in_ring(aux, lax.rem(row + grid_rows - 1, grid_rows))
    relays = core == relay_pair
    up_outer = place_in_ring(aux, up * 2 // ROW_FRAGS)[3]
    down_outer = place_in_ring(aux, down * 2 // ROW_FRAGS)[3]

    ins = [
        pltpu.make_async_copy(there, here, in_sems.at[n])
        for n, (there, here) in enumerate(
            (
                (offset_in, offset),
                (occ_energy_in, occ_energy),
                (vir_energy_in, vir_energy),
                (occ_count_in, occ_count),
                (vir_count_in, vir_count),
            )
        )
    ]
    for copy in ins:
        copy.start()

    barrier = pltpu.get_barrier_semaphore()
    greeted = [(sibling, aux)]
    greeted += [(chip * 2 + n, other) for other in (mate, outer) for n in range(2)]
    greeted += [(up * 2 + n, other) for other in (aux, outer, up_outer) for n in range(2)]
    greeted += [(down * 2 + n, other) for other in (aux, outer, down_outer) for n in range(2)]
    greeted += [(next_row, aux), (next_row, mate), (last_row, aux), (last_row, relay_to)]
    for there, other in greeted:
        pl.semaphore_signal(barrier, inc=1, device_id={"frag": there, "aux": other}, device_id_type=MESH)
    pl.semaphore_wait(barrier, len(greeted))

    def rows_of(who):
        return pl.ds(pl.multiple_of(who * rows, 16), rows)

    def two_cols(s):
        return pl.ds(pl.multiple_of(s * 2 * vir, 128), 2 * vir)

    def z_copy(s):
        return to_device(
            blocks.at[0, :, two_cols(s)], a_stage.at[s], z_send.at[s], z_recv.at[s], up * 2 + 1, aux
        )

    def cand_copy(s, slot, n, there):
        src = blocks.at[0, :, two_cols(s)]
        if there is None:
            return pltpu.make_async_copy(src, cand.at[slot, s], cand_recv.at[slot, s])
        return to_device(src, cand.at[slot, s], cand_send.at[n, s], cand_recv.at[slot, s], there, aux)

    def cand_forward(s):
        return to_device(cand.at[2, s], cand.at[1, s], cand_pass.at[s], cand_recv.at[1, s], sibling, aux)

    def a_source(s, core_is, part):
        if core_is == 0:
            return blocks.at[0, :, pl.ds(pl.multiple_of(s * 2 * vir + part * vir, 128), vir)]
        return a_stage.at[s, :, pl.ds(part * vir, vir)]

    def a_own(s, core_is):
        return pltpu.make_async_copy(
            a_source(s, core_is, core_is), a_half.at[s, rows_of(aux)], a_recv.at[0, s]
        )

    def a_copy(s, core_is, part, kind):
        there, other = {0: (sibling, aux), 1: (chip * 2 + part, mate), 2: (chip * 2 + part, outer)}[kind]
        n = 0 if kind == 0 else 1 + part
        return to_device(
            a_source(s, core_is, part),
            a_half.at[s, rows_of(aux)],
            a_send.at[n, s],
            a_recv.at[kind, s],
            there,
            other,
        )

    def a_forward(s):
        here = a_half.at[s, rows_of(outer)]
        return to_device(here, here, a_send.at[3, s], a_recv.at[3, s], frag, mate)

    def a_landing(s, kind, who):
        here = a_half.at[s, rows_of(who)]
        return to_device(here, here, a_send.at[3, s], a_recv.at[kind, s], frag, mate)

    def begin_a(s):
        for core_is in range(2):
            @pl.when(core == core_is)
            def _():
                if core_is == 1:
                    z_copy(s).wait_recv()

                @pl.when(member)
                def _():
                    a_copy(s, core_is, 0, 1).start()
                    a_copy(s, core_is, 1, 1).start()
                    a_copy(s, core_is, 1 - core_is, 0).start()
                    a_own(s, core_is).start()

                @pl.when(stranger)
                def _():
                    a_copy(s, core_is, 0, 2).start()
                    a_copy(s, core_is, 1, 2).start()

    def b_round(s):
        return to_device(b_other.at[s], relay.at[s], b_send.at[0, s], relay_recv.at[s], next_row, aux)

    def b_relay(s):
        return to_device(
            relay.at[s], b_half.at[s, rows_of(aux)], b_send.at[2, s], b_recv.at[1, s], last_row, relay_to
        )

    def b_outer(s):
        return to_device(
            b_other.at[s], b_half.at[s, rows_of(aux)], b_send.at[0, s], b_recv.at[2, s], frag, outer
        )

    def b_through(s):
        return to_device(b_mine.at[s], transit.at[s], b_send.at[1, s], b_recv.at[0, s], frag, outer)

    def b_forward(s):
        return to_device(
            transit.at[s], b_half.at[s, rows_of(outer)], b_send.at[1, s], b_recv.at[3, s], frag, mate
        )

    def b_landing(s, kind, who):
        here = b_half.at[s, rows_of(who)]
        return to_device(here, here, b_share.at[kind, s], b_recv.at[kind, s], sibling, aux)

    def chosen(s, which):
        cols = pl.ds(pl.multiple_of(which * vir, 128), vir)
        one, two, three = (cand[n, s, :, cols] for n in range(3))
        return jnp.where(chosen_at == 1, one, jnp.where(chosen_at == 2, two, three))

    def begin_b(s):
        @pl.when(core == 1)
        def _():
            cand_copy(s, 2, 1, down * 2).wait_recv()
            cand_forward(s).start()
            cand_copy(s, 0, 0, sibling).wait_recv()
            cand_copy(s, 1, 0, None).wait()

        @pl.when(core == 0)
        def _():
            cand_copy(s, 0, 0, sibling).wait_recv()
            cand_copy(s, 2, 1, down * 2 + 1).wait_recv()
            cand_forward(s).wait_recv()

        b_other[s] = chosen(s, 1 - q_half)

        @pl.when(member)
        def _():
            b_round(s).start()
            b_half[s, rows_of(aux), :] = chosen(s, q_half)
            b_landing(s, 0, aux).start()

        @pl.when(stranger)
        def _():
            b_outer(s).start()
            b_mine[s] = chosen(s, q_half)
            b_through(s).start()

    def pass_on(s):
        a_landing(s, 2, outer).wait_recv()
        a_forward(s).start()

        @pl.when(member)
        def _():
            b_through(s).wait_recv()
            b_forward(s).start()

        @pl.when(relays)
        def _():
            b_round(s).wait_recv()
            b_relay(s).start()

    def gather(s):
        @pl.when(member)
        def _():
            for kind, who in ((2, outer), (1, mate), (3, far)):
                b_landing(s, kind, who).wait_recv()
                b_landing(s, kind, who).start()
            for core_is in range(2):
                @pl.when(core == core_is)
                def _():
                    a_own(s, core_is).wait()

        @pl.when(stranger)
        def _():
            a_landing(s, 0, aux).wait_recv()
            for kind, who in ((0, aux), (2, outer), (1, mate), (3, far)):
                b_landing(s, kind, who).wait_recv()

        a_landing(s, 1, mate).wait_recv()
        a_landing(s, 3, far).wait_recv()

    ins[0].wait()

    @pl.when(core == 1)
    def _():
        @pl.loop(0, steps)
        def _(s):
            z_copy(s).start()

    @pl.loop(0, steps)
    def _(s):
        @pl.when(core == 0)
        def _():
            cand_copy(s, 2, 1, down * 2 + 1).start()
            cand_copy(s, 0, 0, sibling).start()

        @pl.when(core == 1)
        def _():
            cand_copy(s, 2, 1, down * 2).start()
            cand_copy(s, 0, 0, sibling).start()
            cand_copy(s, 1, 0, None).start()

    def off_copy(n):
        if n == 0:
            return to_device(
                off_vectors.at[0], off_vectors.at[1], off_sems.at[0], off_sems.at[1], up * 2 + 1, aux
            )
        return to_device(off_vectors.at[1], off_vectors.at[2], off_sems.at[2], off_sems.at[3], sibling, aux)

    def off_read(n):
        return pltpu.make_async_copy(off_vectors.at[n], off_scalars.at[n - 1], off_sems.at[3 + n])

    own_offset = jnp.full(off_vectors.shape[1:], offset[0], jnp.int32)

    @pl.when(core == 0)
    def _():
        off_vectors[1] = own_offset

    @pl.when(core == 1)
    def _():
        off_vectors[0] = own_offset
        off_copy(0).start()

    begin_a(0)

    @pl.when(core == 1)
    def _():
        off_copy(0).wait()

    @pl.when(member)
    def _():
        off_copy(1).start()
        off_vectors[2] = off_vectors[1]

    off_read(1).start()
    off_read(1).wait()
    chosen_at = off_scalars[0, 0, 0]
    begin_b(0)

    @pl.when(member)
    def _():
        off_copy(1).wait_send()

    @pl.when(stranger)
    def _():
        off_copy(1).wait_recv()

    off_read(2).start()
    for n in range(1, LEAD):
        begin_a(n)
        begin_b(n)

    if padded > 4 * rows:
        for half in (a_half, b_half):
            @pl.loop(0, steps)
            def _(s):
                half[s, 4 * rows :, :] = jnp.zeros((padded - 4 * rows, vir), jnp.bfloat16)

    off_read(2).wait()
    distance = off_scalars[1, 0, 0]
    for copy in ins[1:]:
        copy.wait()
    leader = jnp.where(pair == 0, chip * 2, lax.rem(chip * 2 + frag_total - 1, frag_total))
    partner = jnp.minimum(leader + distance, frag_total - 1)
    valid = leader + distance < frag_total
    leader_occ = occ_count[leader]
    partner_occ = occ_count[partner]
    leader_vir = vir_count[leader]
    partner_vir = vir_count[partner]

    leader_levels = vir_energy[pl.ds(leader, 1), :]
    partner_levels = vir_energy[pl.ds(partner, 1), :]
    row_ids = lax.broadcasted_iota(jnp.int32, (vir, vir), 0)
    col_ids = lax.broadcasted_iota(jnp.int32, (vir, vir), 1)
    base[0] = -leader_levels - jnp.broadcast_to(partner_levels, (vir, vir)).T
    base[1] = -partner_levels - jnp.broadcast_to(leader_levels, (vir, vir)).T
    keep[0] = jnp.where((row_ids < partner_vir) & (col_ids < leader_vir), 1.0, 0.0)
    keep[1] = jnp.where((row_ids < leader_vir) & (col_ids < partner_vir), 1.0, 0.0)
    total[...] = jnp.zeros(total.shape, jnp.float32)
    pass_on(0)

    def tile(i, j, way):
        lead_occ = 2 * i + core
        part_occ = 2 * j + q_half
        ok = jnp.logical_and(valid, jnp.logical_and(lead_occ < leader_occ, part_occ < partner_occ))
        level = occ_energy[lead_occ, leader] + occ_energy[part_occ, partner]
        turned, straight = (b_turned, a_half.at[i]) if way == 0 else (a_turned, b_half.at[j])
        integrals = jnp.dot(turned[...], straight[...], preferred_element_type=jnp.float32)
        amplitude = integrals * (keep[way] * jnp.where(ok, 1.0, 0.0)) / (base[way] + level)
        energy = amplitude * integrals
        rounded = amplitude.astype(jnp.bfloat16)
        of_cols = lax.dot_general(
            rounded, rounded, (((0,), (0,)), ((), ())), preferred_element_type=jnp.float32
        )
        of_rows = lax.dot_general(
            rounded, rounded, (((1,), (1,)), ((), ())), preferred_element_type=jnp.float32
        )
        first, second = (of_cols, of_rows) if way == 0 else (of_rows, of_cols)
        for n in range(4):
            piece = slice(n * aux_rows, (n + 1) * aux_rows)
            total[n, :aux_rows, :] += first[piece]
            total[n, aux_rows : 2 * aux_rows, :] += second[piece]
        total[0, 2 * aux_rows :, :] += energy.reshape(vir // 8, 8, vir).sum(0)

    def work(s):
        for at in range(0, padded, BLOCK):
            b_turned[:, at : at + BLOCK] = b_half[s, at : at + BLOCK, :].T
            a_turned[:, at : at + BLOCK] = a_half[s, at : at + BLOCK, :].T

        @pl.loop(0, s + 1)
        def _(i):
            tile(i, s, 0)

        @pl.loop(0, s)
        def _(j):
            tile(s, j, 1)

    @pl.loop(0, steps)
    def _(s):
        @pl.when(s + LEAD < steps)
        def _():
            begin_a(s + LEAD)
            begin_b(s + LEAD)

        @pl.when(s + 1 < steps)
        def _():
            pass_on(s + 1)

        gather(s)
        work(s)

    for n in range(1, 4):
        total[n, 2 * aux_rows :, :] = total[0, 2 * aux_rows :, :]
    column = jnp.where(member, aux, outer)
    who = q_half * 2 + core

    def sum_copy(n, going):
        there, other, quarter, sender = (
            (sibling, aux, jnp.where(member, outer, aux), q_half * 2 + 1 - core),
            (chip * 2 + pair, mate, mate, (1 - q_half) * 2 + pair),
            (chip * 2 + 1 - pair, mate, far, (1 - q_half) * 2 + 1 - pair),
        )[n]
        slot = who if going else sender
        return to_device(total.at[quarter], landed.at[slot], sum_send.at[n], sum_recv.at[slot], there, other)

    for n in (1, 2, 0):
        sum_copy(n, True).start()
    landed[who] = total[column]
    for n in (0, 1, 2):
        sum_copy(n, True).wait_send()
        sum_copy(n, False).wait_recv()
    sums = landed[0] + landed[1] + landed[2] + landed[3]
    summed[0, :aux_rows, :] = sums[:aux_rows]
    summed[0, aux_rows:, :] = sums[2 * aux_rows :]
    for n in range(1, 4):
        summed[n, :aux_rows, :] = jnp.where(distance == n, sums[aux_rows : 2 * aux_rows], 0.0)

    def part_copy(n):
        there = (
            jnp.where(pair == 0, chip * 2, down * 2 + 1),
            jnp.where(pair == 0, chip * 2 + 1, chip * 2),
            jnp.where(pair == 0, up * 2, chip * 2 + 1),
            jnp.where(pair == 0, up * 2 + 1, up * 2),
        )[n]
        if n == 0:
            src, dst = summed.at[0], parts.at[0]
        else:
            src, dst = summed.at[n, pl.ds(0, aux_rows)], parts.at[n, pl.ds(0, aux_rows)]
        return to_device(src, dst, part_send.at[n], part_recv.at[n], there, column)

    for n in (0, 2):
        stays = jnp.logical_and(member, core == n // 2)

        @pl.when(jnp.logical_not(stays))
        def _():
            part_copy(n).start()

        @pl.when(stays)
        def _():
            parts[n] = summed[n]

    for n in (1, 3):
        part_copy(n).start()
    for n in (1, 3):
        part_copy(n).wait()
    for n in (0, 2):
        stays = jnp.logical_and(member, core == n // 2)

        @pl.when(jnp.logical_not(stays))
        def _():
            part_copy(n).wait()

    density_out[0] = (
        parts[0, :aux_rows, :] + parts[1, :aux_rows, :] + parts[2, :aux_rows, :] + parts[3, :aux_rows, :]
    )
    energy_out[0] = jnp.sum(parts[0, aux_rows:, :])

    @pl.loop(0, steps)
    def _(s):
        cand_copy(s, 0, 0, sibling).wait_send()
        cand_copy(s, 2, 1, sibling).wait_send()
        a_forward(s).wait_send()
        for core_is in range(2):
            @pl.when(core == core_is)
            def _():
                a_copy(s, core_is, 0, 1).wait_send()
                a_copy(s, core_is, 1, 1).wait_send()

                @pl.when(member)
                def _():
                    a_copy(s, core_is, 1 - core_is, 0).wait_send()

        @pl.when(core == 1)
        def _():
            z_copy(s).wait_send()
            cand_forward(s).wait_send()

        @pl.when(member)
        def _():
            for kind, who_is in enumerate((aux, mate, outer, far)):
                b_landing(s, kind, who_is).wait_send()

        b_round(s).wait_send()
        b_through(s).wait_send()

        @pl.when(relays)
        def _():
            b_relay(s).wait_send()


def on_device(blocks, occ_energy, vir_energy, occ_count, vir_count, partner_offset):
    frag_total, occ = occ_energy.shape
    vir = vir_energy.shape[1]
    rows = blocks.shape[1]
    steps = occ // 2
    padded = -(-4 * rows // BLOCK) * BLOCK
    aux_rows = vir // 4
    vmem = pl.BlockSpec(memory_space=pltpu.VMEM)
    smem = pl.BlockSpec(memory_space=pltpu.SMEM)
    anywhere = pl.BlockSpec(memory_space=pl.ANY)
    dma = pltpu.SemaphoreType.DMA
    results = pl.pallas_call(
        functools.partial(kernel, frag_total),
        out_shape=(
            jax.ShapeDtypeStruct((1,), jnp.float32),
            jax.ShapeDtypeStruct((1, aux_rows, vir), jnp.float32),
            jax.ShapeDtypeStruct((steps, rows, 2 * vir), jnp.bfloat16),
            jax.ShapeDtypeStruct((steps, rows, vir), jnp.bfloat16),
            jax.ShapeDtypeStruct((steps, rows, vir), jnp.bfloat16),
        ),
        in_specs=[anywhere] * 6,
        out_specs=(smem, vmem, anywhere, anywhere, anywhere),
        scratch_shapes=[
            pltpu.SMEM((occ, frag_total), jnp.float32),
            pltpu.VMEM((frag_total, vir), jnp.float32),
            pltpu.SMEM((frag_total,), jnp.int32),
            pltpu.SMEM((frag_total,), jnp.int32),
            pltpu.SMEM((1,), jnp.int32),
            pltpu.VMEM((steps, padded, vir), jnp.bfloat16),
            pltpu.VMEM((steps, padded, vir), jnp.bfloat16),
            pltpu.VMEM((steps, rows, vir), jnp.bfloat16),
            pltpu.VMEM((steps, rows, vir), jnp.bfloat16),
            pltpu.VMEM((3, steps, rows, 2 * vir), jnp.bfloat16),
            pltpu.VMEM((vir, padded), jnp.bfloat16),
            pltpu.VMEM((vir, padded), jnp.bfloat16),
            pltpu.VMEM((2, vir, vir), jnp.float32),
            pltpu.VMEM((2, vir, vir), jnp.float32),
            pltpu.VMEM((4, 2 * aux_rows + 8, vir), jnp.float32),
            pltpu.VMEM((4, 2 * aux_rows + 8, vir), jnp.float32),
            pltpu.VMEM((4, aux_rows + 8, vir), jnp.float32),
            pltpu.VMEM((4, aux_rows + 8, vir), jnp.float32),
            pltpu.VMEM((3, 8, 128), jnp.int32),
            pltpu.SMEM((2, 8, 128), jnp.int32),
            dma((5,)),
            dma((steps,)),
            dma((steps,)),
            dma((4, steps)),
            dma((4, steps)),
            dma((2, steps)),
            dma((3, steps)),
            dma((steps,)),
            dma((3, steps)),
            dma((4, steps)),
            dma((4, steps)),
            dma((steps,)),
            dma((6,)),
            dma((3,)),
            dma((4,)),
            dma((4,)),
            dma((4,)),
        ],
        compiler_params=pltpu.CompilerParams(
            collective_id=0, has_side_effects=True, vmem_limit_bytes=60 * 1024 * 1024
        ),
        cost_estimate=pl.CostEstimate(
            flops=2 * 4 * rows * (occ * vir // 2) ** 2, bytes_accessed=2 * rows * occ * vir, transcendentals=0
        ),
        name="pair_terms",
    )(blocks, occ_energy.T, vir_energy, occ_count, vir_count, partner_offset)
    return results[0], results[1]


def solution(mesh):
    placed = (P("frag", "aux", None), P(), P(), P(), P(), P("frag"))
    return jax.shard_map(
        on_device,
        mesh=mesh,
        in_specs=placed,
        out_specs=(P("frag"), P("frag", "aux", None)),
        check_vma=False,
    )
```

time: 789 us -> 289 us (0.37)
  waiting for transfers between devices: 616 us -> 0 us
  Pallas kernels: 0 us -> 284 us
  starting transfers between devices: 53.7 us -> 0 us
  matrix products: 50.6 us -> 0 us
  local copies, waits for them, and re-layouts: 32.5 us -> 1.47 us
  between operations: 14.9 us -> 2.98 us
  other arithmetic: 11.1 us -> 0 us
  blocking collectives: 7.93 us -> 0 us
    all_gather x1 -> x0, waiting for transfers between devices: 360 us -> none  [on_device(): lax.all_gather(partner_block, 'aux', axis=0, tiled=True)]
    pallas_call x0 -> x1, Pallas kernels: none -> 284 us  [on_device(): pl.pallas_call(functools.partial(kernel, frag_total), out_shape=(jax.Shap...]
    ppermute x6 -> x0, waiting for transfers between devices: 207 us -> none  [passed_along(): return lax.ppermute(array, axis, pairs)]
    dot_general x3 -> x0, matrix products: 50.6 us -> none  [the longest x1 39.2 us: on_device(): lax.dot_general(own_rows, lax.all_gather(partner_block, 'aux', axis=0, ti...]
    ppermute x6 -> x0, starting transfers between devices: 48.1 us -> none  [passed_along(): return lax.ppermute(array, axis, pairs)]
    all_to_all x1 -> x0, waiting for transfers between devices: 32.2 us -> none  [on_device(): lax.all_to_all(own_block, 'aux', split_axis=1, concat_axis=0, tiled=True)]
    reduce_scatter x1 -> x0, waiting for transfers between devices: 17 us -> none  [on_device(): lax.psum_scatter(collected, 'aux', scatter_dimension=0, tiled=True)]
    reshape x1 -> x0, local copies, waits for them, and re-layouts: 13.5 us -> none  [on_device(): by_column = amp_half.reshape(row_count * occ_width, vir_width)]
  transfers between devices with their start and end apart: 9 -> 0, of which waited for: 7 -> 0; matrix products, arithmetic and copies ran while one was open for 3% -> 0% of each run, Pallas kernels for 0% -> 0%
where the time goes in v2:
time: 289 us
  Pallas kernels  284 us (98%)
  between operations  2.98 us (1%)
    pallas_call x1, Pallas kernels, on_device(): pl.pallas_call(functools.partial(kernel, frag_total), out_shape=(jax.Shap...  284 us

profile of v2, /device:TPU:1, one launch (start us, length us, event | category | flops | bytes accessed | tf_op | source)
XLA Modules:
  0.0 288.8 jit_solution(12404208792116064601)
XLA Ops:
  1.3 284.4 %pair_terms.1 = (f32[1]{0:T(128)}, f32[1,64,256]{2,1,0:T(8,128)}, bf16[8,752,512]{2,1,0:T(8,128)(2,1)}, bf16[8,752,256]{2,1,0:T(8,128)(2,1)}, bf16[8,752,256]{2,1,0:T(8,128)(2,1)}) custom-call(bf16[1,752,4096]{2,1,0:T(8,128)(2,1)} %blocks.1, f32[16,32]{1,0:T(8,128)} %bitcast.1, f32[32,256]{1,0:T(8,128)} %vir_energy_in.1, s32[32]{0:T(128)} %occ_count_in.1, ...), custom_call_target="tpu_custom_call" | custom-call | flops 25232932864 | bytes 6160384 | tf_op jit(solution)/shard_map/pair_terms/pallas_call | solution.py:558
  286.2 1.5 copy.12

commit v3 on v2

--- a/solution.py
+++ b/solution.py
@@ -7,7 +7,35 @@
 from jax.experimental.pallas import tpu as pltpu
 from jax.sharding import PartitionSpec as P
 
-LEAD = 2
+START = (
+    ("z_up", 0),
+    ("z_down", 0),
+    ("a", 0),
+    ("z_up", 1),
+    ("a", 1),
+    ("z_up", 2),
+    ("b", 0),
+    ("z_down", 1),
+    ("pass_a", 0),
+    ("a", 2),
+    ("z_up", 3),
+    ("z_down", 2),
+    ("b", 1),
+    ("pass_a", 1),
+    ("pass_b", 0),
+    ("gather_a", 0),
+)
+ORDER = (
+    ("z_up", 4),
+    ("a", 3),
+    ("z_down", 3),
+    ("b", 2),
+    ("pass_b", 1),
+    ("pass_a", 2),
+    ("gather_a", 1),
+    ("gather_b", 0),
+    ("work", 0),
+)
 BLOCK = 256
 ROW_FRAGS = 8
 MESH = pl.DeviceIdType.MESH
@@ -154,6 +182,23 @@
     def cand_forward(s):
         return to_device(cand.at[2, s], cand.at[1, s], cand_pass.at[s], cand_recv.at[1, s], sibling, aux)
 
+    def z_up(s):
+        @pl.when(core == 1)
+        def _():
+            z_copy(s).start()
+
+    def z_down(s):
+        @pl.when(core == 0)
+        def _():
+            cand_copy(s, 2, 1, down * 2 + 1).start()
+            cand_copy(s, 0, 0, sibling).start()
+
+        @pl.when(core == 1)
+        def _():
+            cand_copy(s, 2, 1, down * 2).start()
+            cand_copy(s, 0, 0, sibling).start()
+            cand_copy(s, 1, 0, None).start()
+
     def a_source(s, core_is, part):
         if core_is == 0:
             return blocks.at[0, :, pl.ds(pl.multiple_of(s * 2 * vir + part * vir, 128), vir)]
@@ -231,6 +276,7 @@
     def chosen(s, which):
         cols = pl.ds(pl.multiple_of(which * vir, 128), vir)
         one, two, three = (cand[n, s, :, cols] for n in range(3))
+        chosen_at = off_scalars[0, 0, 0]
         return jnp.where(chosen_at == 1, one, jnp.where(chosen_at == 2, two, three))
 
     def begin_b(s):
@@ -261,10 +307,11 @@
             b_mine[s] = chosen(s, q_half)
             b_through(s).start()
 
-    def pass_on(s):
+    def pass_a(s):
         a_landing(s, 2, outer).wait_recv()
         a_forward(s).start()
 
+    def pass_b(s):
         @pl.when(member)
         def _():
             b_through(s).wait_recv()
@@ -275,12 +322,9 @@
             b_round(s).wait_recv()
             b_relay(s).start()
 
-    def gather(s):
+    def gather_a(s):
         @pl.when(member)
         def _():
-            for kind, who in ((2, outer), (1, mate), (3, far)):
-                b_landing(s, kind, who).wait_recv()
-                b_landing(s, kind, who).start()
             for core_is in range(2):
                 @pl.when(core == core_is)
                 def _():
@@ -289,32 +333,23 @@
         @pl.when(stranger)
         def _():
             a_landing(s, 0, aux).wait_recv()
+
+        a_landing(s, 1, mate).wait_recv()
+        a_landing(s, 3, far).wait_recv()
+
+    def gather_b(s):
+        @pl.when(member)
+        def _():
+            for kind, who in ((2, outer), (1, mate), (3, far)):
+                b_landing(s, kind, who).wait_recv()
+                b_landing(s, kind, who).start()
+
+        @pl.when(stranger)
+        def _():
             for kind, who in ((0, aux), (2, outer), (1, mate), (3, far)):
                 b_landing(s, kind, who).wait_recv()
 
-        a_landing(s, 1, mate).wait_recv()
-        a_landing(s, 3, far).wait_recv()
-
     ins[0].wait()
-
-    @pl.when(core == 1)
-    def _():
-        @pl.loop(0, steps)
-        def _(s):
-            z_copy(s).start()
-
-    @pl.loop(0, steps)
-    def _(s):
-        @pl.when(core == 0)
-        def _():
-            cand_copy(s, 2, 1, down * 2 + 1).start()
-            cand_copy(s, 0, 0, sibling).start()
-
-        @pl.when(core == 1)
-        def _():
-            cand_copy(s, 2, 1, down * 2).start()
-            cand_copy(s, 0, 0, sibling).start()
-            cand_copy(s, 1, 0, None).start()
 
     def off_copy(n):
         if n == 0:
@@ -337,21 +372,33 @@
         off_vectors[0] = own_offset
         off_copy(0).start()
 
-    begin_a(0)
-
-    @pl.when(core == 1)
-    def _():
-        off_copy(0).wait()
-
-    @pl.when(member)
-    def _():
-        off_copy(1).start()
-        off_vectors[2] = off_vectors[1]
-
-    off_read(1).start()
-    off_read(1).wait()
-    chosen_at = off_scalars[0, 0, 0]
-    begin_b(0)
+    def know_offsets():
+        @pl.when(core == 1)
+        def _():
+            off_copy(0).wait()
+
+        @pl.when(member)
+        def _():
+            off_copy(1).start()
+            off_vectors[2] = off_vectors[1]
+
+        off_read(1).start()
+        off_read(1).wait()
+
+    stages = {
+        "z_up": z_up,
+        "z_down": z_down,
+        "a": begin_a,
+        "b": begin_b,
+        "pass_a": pass_a,
+        "pass_b": pass_b,
+        "gather_a": gather_a,
+        "gather_b": gather_b,
+    }
+    for name, n in START:
+        if (name, n) == ("b", 0):
+            know_offsets()
+        stages[name](n)
 
     @pl.when(member)
     def _():
@@ -362,10 +409,6 @@
         off_copy(1).wait_recv()
 
     off_read(2).start()
-    for n in range(1, LEAD):
-        begin_a(n)
-        begin_b(n)
-
     if padded > 4 * rows:
         for half in (a_half, b_half):
             @pl.loop(0, steps)
@@ -393,7 +436,6 @@
     keep[0] = jnp.where((row_ids < partner_vir) & (col_ids < leader_vir), 1.0, 0.0)
     keep[1] = jnp.where((row_ids < leader_vir) & (col_ids < partner_vir), 1.0, 0.0)
     total[...] = jnp.zeros(total.shape, jnp.float32)
-    pass_on(0)
 
     def tile(i, j, way):
         lead_occ = 2 * i + core
@@ -419,31 +461,42 @@
         total[0, 2 * aux_rows :, :] += energy.reshape(vir // 8, 8, vir).sum(0)
 
     def work(s):
+        ahead = s + 1 < steps
         for at in range(0, padded, BLOCK):
             b_turned[:, at : at + BLOCK] = b_half[s, at : at + BLOCK, :].T
-            a_turned[:, at : at + BLOCK] = a_half[s, at : at + BLOCK, :].T
-
-        @pl.loop(0, s + 1)
-        def _(i):
-            tile(i, s, 0)
-
-        @pl.loop(0, s)
-        def _(j):
-            tile(s, j, 1)
+        columns = jnp.minimum(s + 2, steps)
+
+        @pl.loop(0, columns // 2)
+        def _(n):
+            tile(2 * n, s, 0)
+            tile(2 * n + 1, s, 0)
+
+        @pl.when(lax.rem(columns, 2) == 1)
+        def _():
+            tile(columns - 1, s, 0)
+
+        @pl.when(ahead)
+        def _():
+            for at in range(0, padded, BLOCK):
+                a_turned[:, at : at + BLOCK] = a_half[s + 1, at : at + BLOCK, :].T
+
+            @pl.loop(0, s // 2)
+            def _(n):
+                tile(s + 1, 2 * n, 1)
+                tile(s + 1, 2 * n + 1, 1)
+
+            @pl.when(lax.rem(s, 2) == 1)
+            def _():
+                tile(s + 1, s - 1, 1)
+
+    stages["work"] = work
 
     @pl.loop(0, steps)
     def _(s):
-        @pl.when(s + LEAD < steps)
-        def _():
-            begin_a(s + LEAD)
-            begin_b(s + LEAD)
-
-        @pl.when(s + 1 < steps)
-        def _():
-            pass_on(s + 1)
-
-        gather(s)
-        work(s)
+        for name, lead in ORDER:
+            @pl.when(s + lead < steps)
+            def _():
+                stages[name](s + lead)
 
     for n in range(1, 4):
         total[n, 2 * aux_rows :, :] = total[0, 2 * aux_rows :, :]

time: 289 us -> 230 us (0.80)
  Pallas kernels: 284 us -> 225 us
    pallas_call x1, Pallas kernels: 284 us -> 225 us  [on_device(): pl.pallas_call(functools.partial(kernel, frag_total), out_shape=(jax.Shap...]
where the time goes in v3:
time: 230 us
  Pallas kernels  225 us (98%)
  between operations  2.98 us (1%)
    pallas_call x1, Pallas kernels, on_device(): pl.pallas_call(functools.partial(kernel, frag_total), out_shape=(jax.Shap...  225 us

profile of v3, /device:TPU:1, one launch (start us, length us, event | category | flops | bytes accessed | tf_op | source)
XLA Modules:
  0.0 229.8 jit_solution(2945737362034918168)
XLA Ops:
  1.3 225.4 %pair_terms.1 = (f32[1]{0:T(128)}, f32[1,64,256]{2,1,0:T(8,128)}, bf16[8,752,512]{2,1,0:T(8,128)(2,1)}, bf16[8,752,256]{2,1,0:T(8,128)(2,1)}, bf16[8,752,256]{2,1,0:T(8,128)(2,1)}) custom-call(bf16[1,752,4096]{2,1,0:T(8,128)(2,1)} %blocks.1, f32[16,32]{1,0:T(8,128)} %bitcast.1, f32[32,256]{1,0:T(8,128)} %vir_energy_in.1, s32[32]{0:T(128)} %occ_count_in.1, ...), custom_call_target="tpu_custom_call" | custom-call | flops 25232932864 | bytes 6160384 | tf_op jit(solution)/shard_map/pair_terms/pallas_call | solution.py:611
  227.2 1.5 copy.12

commit v4 on v3

--- a/solution.py
+++ b/solution.py
@@ -10,31 +10,33 @@
 START = (
     ("z_up", 0),
     ("z_down", 0),
+    ("z_down", 1),
     ("a", 0),
     ("z_up", 1),
     ("a", 1),
     ("z_up", 2),
+    ("pass_a", 0),
     ("b", 0),
-    ("z_down", 1),
-    ("pass_a", 0),
+    ("z_down", 2),
     ("a", 2),
     ("z_up", 3),
-    ("z_down", 2),
+    ("pass_a", 1),
     ("b", 1),
-    ("pass_a", 1),
+    ("z_down", 3),
     ("pass_b", 0),
     ("gather_a", 0),
 )
 ORDER = (
     ("z_up", 4),
     ("a", 3),
-    ("z_down", 3),
     ("b", 2),
+    ("z_down", 4),
     ("pass_b", 1),
     ("pass_a", 2),
     ("gather_a", 1),
     ("gather_b", 0),
-    ("work", 0),
+    ("columns", 0),
+    ("across", 0),
 )
 BLOCK = 256
 ROW_FRAGS = 8
@@ -87,6 +89,7 @@
     b_turned,
     base,
     keep,
+    halves,
     total,
     landed,
     summed,
@@ -134,8 +137,6 @@
     stranger = core != pair
     relay_pair, _, relay_to, _ = place_in_ring(aux, lax.rem(row + grid_rows - 1, grid_rows))
     relays = core == relay_pair
-    up_outer = place_in_ring(aux, up * 2 // ROW_FRAGS)[3]
-    down_outer = place_in_ring(aux, down * 2 // ROW_FRAGS)[3]
 
     ins = [
         pltpu.make_async_copy(there, here, in_sems.at[n])
@@ -154,9 +155,8 @@
 
     barrier = pltpu.get_barrier_semaphore()
     greeted = [(sibling, aux)]
-    greeted += [(chip * 2 + n, other) for other in (mate, outer) for n in range(2)]
-    greeted += [(up * 2 + n, other) for other in (aux, outer, up_outer) for n in range(2)]
-    greeted += [(down * 2 + n, other) for other in (aux, outer, down_outer) for n in range(2)]
+    greeted += [(chip * 2 + n, other) for other in (mate, outer, far) for n in range(2)]
+    greeted += [(there * 2 + n, aux) for there in (up, down) for n in range(2)]
     greeted += [(next_row, aux), (next_row, mate), (last_row, aux), (last_row, relay_to)]
     for there, other in greeted:
         pl.semaphore_signal(barrier, inc=1, device_id={"frag": there, "aux": other}, device_id_type=MESH)
@@ -437,7 +437,7 @@
     keep[1] = jnp.where((row_ids < leader_vir) & (col_ids < partner_vir), 1.0, 0.0)
     total[...] = jnp.zeros(total.shape, jnp.float32)
 
-    def tile(i, j, way):
+    def amplitudes(i, j, way):
         lead_occ = 2 * i + core
         part_occ = 2 * j + q_half
         ok = jnp.logical_and(valid, jnp.logical_and(lead_occ < leader_occ, part_occ < partner_occ))
@@ -446,50 +446,54 @@
         integrals = jnp.dot(turned[...], straight[...], preferred_element_type=jnp.float32)
         amplitude = integrals * (keep[way] * jnp.where(ok, 1.0, 0.0)) / (base[way] + level)
         energy = amplitude * integrals
-        rounded = amplitude.astype(jnp.bfloat16)
-        of_cols = lax.dot_general(
-            rounded, rounded, (((0,), (0,)), ((), ())), preferred_element_type=jnp.float32
-        )
-        of_rows = lax.dot_general(
-            rounded, rounded, (((1,), (1,)), ((), ())), preferred_element_type=jnp.float32
-        )
+        total[0, 2 * aux_rows :, :] += energy.reshape(vir // 8, 8, vir).sum(0)
+        return amplitude.astype(jnp.bfloat16)
+
+    def squares(rounded, way):
+        of_cols, of_rows = 0.0, 0.0
+        for each in rounded:
+            of_cols += lax.dot_general(each, each, (((0,), (0,)), ((), ())), preferred_element_type=jnp.float32)
+            of_rows += lax.dot_general(each, each, (((1,), (1,)), ((), ())), preferred_element_type=jnp.float32)
         first, second = (of_cols, of_rows) if way == 0 else (of_rows, of_cols)
         for n in range(4):
             piece = slice(n * aux_rows, (n + 1) * aux_rows)
             total[n, :aux_rows, :] += first[piece]
             total[n, aux_rows : 2 * aux_rows, :] += second[piece]
-        total[0, 2 * aux_rows :, :] += energy.reshape(vir // 8, 8, vir).sum(0)
-
-    def work(s):
-        ahead = s + 1 < steps
+
+    def tiles(count, way, place):
+        def two(n):
+            for m in range(2):
+                halves[m] = amplitudes(*place(2 * n + m), way)
+
+        @pl.when(count > 1)
+        def _():
+            two(0)
+
+            @pl.loop(1, count // 2)
+            def _(n):
+                squares([halves[m] for m in range(2)], way)
+                two(n)
+
+            squares([halves[m] for m in range(2)], way)
+
+        @pl.when(lax.rem(count, 2) == 1)
+        def _():
+            squares([amplitudes(*place(count - 1), way)], way)
+
+    def columns(s):
         for at in range(0, padded, BLOCK):
             b_turned[:, at : at + BLOCK] = b_half[s, at : at + BLOCK, :].T
-        columns = jnp.minimum(s + 2, steps)
-
-        @pl.loop(0, columns // 2)
-        def _(n):
-            tile(2 * n, s, 0)
-            tile(2 * n + 1, s, 0)
-
-        @pl.when(lax.rem(columns, 2) == 1)
-        def _():
-            tile(columns - 1, s, 0)
-
-        @pl.when(ahead)
+        tiles(jnp.minimum(s + 2, steps), 0, lambda n: (n, s))
+
+    def across(s):
+        @pl.when(s + 1 < steps)
         def _():
             for at in range(0, padded, BLOCK):
                 a_turned[:, at : at + BLOCK] = a_half[s + 1, at : at + BLOCK, :].T
-
-            @pl.loop(0, s // 2)
-            def _(n):
-                tile(s + 1, 2 * n, 1)
-                tile(s + 1, 2 * n + 1, 1)
-
-            @pl.when(lax.rem(s, 2) == 1)
-            def _():
-                tile(s + 1, s - 1, 1)
-
-    stages["work"] = work
+            tiles(s, 1, lambda n: (s + 1, n))
+
+    stages["columns"] = columns
+    stages["across"] = across
 
     @pl.loop(0, steps)
     def _(s):
@@ -500,69 +504,26 @@
 
     for n in range(1, 4):
         total[n, 2 * aux_rows :, :] = total[0, 2 * aux_rows :, :]
-    column = jnp.where(member, aux, outer)
     who = q_half * 2 + core
 
-    def sum_copy(n, going):
-        there, other, quarter, sender = (
-            (sibling, aux, jnp.where(member, outer, aux), q_half * 2 + 1 - core),
-            (chip * 2 + pair, mate, mate, (1 - q_half) * 2 + pair),
-            (chip * 2 + 1 - pair, mate, far, (1 - q_half) * 2 + 1 - pair),
-        )[n]
-        slot = who if going else sender
-        return to_device(total.at[quarter], landed.at[slot], sum_send.at[n], sum_recv.at[slot], there, other)
-
-    for n in (1, 2, 0):
-        sum_copy(n, True).start()
-    landed[who] = total[column]
-    for n in (0, 1, 2):
-        sum_copy(n, True).wait_send()
-        sum_copy(n, False).wait_recv()
-    sums = landed[0] + landed[1] + landed[2] + landed[3]
-    summed[0, :aux_rows, :] = sums[:aux_rows]
-    summed[0, aux_rows:, :] = sums[2 * aux_rows :]
-    for n in range(1, 4):
-        summed[n, :aux_rows, :] = jnp.where(distance == n, sums[aux_rows : 2 * aux_rows], 0.0)
-
-    def part_copy(n):
-        there = (
-            jnp.where(pair == 0, chip * 2, down * 2 + 1),
-            jnp.where(pair == 0, chip * 2 + 1, chip * 2),
-            jnp.where(pair == 0, up * 2, chip * 2 + 1),
-            jnp.where(pair == 0, up * 2 + 1, up * 2),
-        )[n]
-        if n == 0:
-            src, dst = summed.at[0], parts.at[0]
-        else:
-            src, dst = summed.at[n, pl.ds(0, aux_rows)], parts.at[n, pl.ds(0, aux_rows)]
-        return to_device(src, dst, part_send.at[n], part_recv.at[n], there, column)
-
-    for n in (0, 2):
-        stays = jnp.logical_and(member, core == n // 2)
-
-        @pl.when(jnp.logical_not(stays))
-        def _():
-            part_copy(n).start()
-
-        @pl.when(stays)
-        def _():
-            parts[n] = summed[n]
-
-    for n in (1, 3):
-        part_copy(n).start()
-    for n in (1, 3):
-        part_copy(n).wait()
-    for n in (0, 2):
-        stays = jnp.logical_and(member, core == n // 2)
-
-        @pl.when(jnp.logical_not(stays))
-        def _():
-            part_copy(n).wait()
-
-    density_out[0] = (
-        parts[0, :aux_rows, :] + parts[1, :aux_rows, :] + parts[2, :aux_rows, :] + parts[3, :aux_rows, :]
-    )
-    energy_out[0] = jnp.sum(parts[0, aux_rows:, :])
+    def sum_copy(n):
+        column = lax.rem(aux + n, 4)
+        there = sibling if n == 0 else chip * 2 + pair
+        return to_device(total.at[column], landed.at[who], sum_send.at[n], sum_recv.at[who], there, column)
+
+    def sum_landing(n):
+        return to_device(landed.at[n], landed.at[n], sum_send.at[0], sum_recv.at[n], sibling, aux)
+
+    for n in (2, 1, 3):
+        sum_copy(n).start()
+
+    @pl.when(stranger)
+    def _():
+        sum_copy(0).start()
+
+    @pl.when(member)
+    def _():
+        landed[who] = total[aux]
 
     @pl.loop(0, steps)
     def _(s):
@@ -595,6 +556,65 @@
         @pl.when(relays)
         def _():
             b_relay(s).wait_send()
+
+    for n in range(1, 4):
+        sum_copy(n).wait_send()
+
+    @pl.when(stranger)
+    def _():
+        sum_copy(0).wait_send()
+
+    for n in range(4):
+        @pl.when(jnp.logical_or(stranger, who != n))
+        def _():
+            sum_landing(n).wait_recv()
+
+    own_distance = off_scalars[0, 0, 0]
+    sums = landed[0] + landed[1] + landed[2] + landed[3]
+    summed[0, :aux_rows, :] = sums[:aux_rows]
+    summed[0, aux_rows:, :] = sums[2 * aux_rows :]
+    for n in range(1, 4):
+        summed[n, :aux_rows, :] = jnp.where(own_distance == n, sums[aux_rows : 2 * aux_rows], 0.0)
+
+    def part_copy(n):
+        there = (
+            down * 2 + 1,
+            sibling,
+            up * 2,
+            jnp.where(core == 0, up * 2 + 1, up * 2),
+        )[n]
+        if n == 0:
+            src, dst = summed.at[0], parts.at[0]
+        else:
+            src, dst = summed.at[n, pl.ds(0, aux_rows)], parts.at[n, pl.ds(0, aux_rows)]
+        return to_device(src, dst, part_send.at[n], part_recv.at[n], there, aux)
+
+    for n in (0, 2):
+        stays = core == n // 2
+
+        @pl.when(core != n // 2)
+        def _():
+            part_copy(n).start()
+
+        @pl.when(stays)
+        def _():
+            parts[n] = summed[n]
+
+    for n in (1, 3):
+        part_copy(n).start()
+    for n in (1, 3):
+        part_copy(n).wait()
+    for n in (0, 2):
+        stays = core == n // 2
+
+        @pl.when(core != n // 2)
+        def _():
+            part_copy(n).wait()
+
+    density_out[0] = (
+        parts[0, :aux_rows, :] + parts[1, :aux_rows, :] + parts[2, :aux_rows, :] + parts[3, :aux_rows, :]
+    )
+    energy_out[0] = jnp.sum(parts[0, aux_rows:, :])
 
 
 def on_device(blocks, occ_energy, vir_energy, occ_count, vir_count, partner_offset):
@@ -634,6 +654,7 @@
             pltpu.VMEM((vir, padded), jnp.bfloat16),
             pltpu.VMEM((2, vir, vir), jnp.float32),
             pltpu.VMEM((2, vir, vir), jnp.float32),
+            pltpu.VMEM((2, vir, vir), jnp.bfloat16),
             pltpu.VMEM((4, 2 * aux_rows + 8, vir), jnp.float32),
             pltpu.VMEM((4, 2 * aux_rows + 8, vir), jnp.float32),
             pltpu.VMEM((4, aux_rows + 8, vir), jnp.float32),
@@ -653,7 +674,7 @@
             dma((4, steps)),
             dma((steps,)),
             dma((6,)),
-            dma((3,)),
+            dma((4,)),
             dma((4,)),
             dma((4,)),
             dma((4,)),

time: 230 us -> 221 us (0.961)
  Pallas kernels: 225 us -> 217 us
    pallas_call x1, Pallas kernels: 225 us -> 217 us  [on_device(): pl.pallas_call(functools.partial(kernel, frag_total), out_shape=(jax.Shap...]
where the time goes in v4:
time: 221 us
  Pallas kernels  217 us (98%)
  between operations  2.98 us (1%)
    pallas_call x1, Pallas kernels, on_device(): pl.pallas_call(functools.partial(kernel, frag_total), out_shape=(jax.Shap...  217 us

profile of v4, /device:TPU:1, one launch (start us, length us, event | category | flops | bytes accessed | tf_op | source)
XLA Modules:
  0.0 221.1 jit_solution(15401793497868782452)
XLA Ops:
  1.3 216.7 %pair_terms.1 = (f32[1]{0:T(128)}, f32[1,64,256]{2,1,0:T(8,128)}, bf16[8,752,512]{2,1,0:T(8,128)(2,1)}, bf16[8,752,256]{2,1,0:T(8,128)(2,1)}, bf16[8,752,256]{2,1,0:T(8,128)(2,1)}) custom-call(bf16[1,752,4096]{2,1,0:T(8,128)(2,1)} %blocks.1, f32[16,32]{1,0:T(8,128)} %bitcast.1, f32[32,256]{1,0:T(8,128)} %vir_energy_in.1, s32[32]{0:T(128)} %occ_count_in.1, ...), custom_call_target="tpu_custom_call" | custom-call | flops 25232932864 | bytes 6160384 | tf_op jit(solution)/shard_map/pair_terms/pallas_call | solution.py:631
  218.5 1.5 copy.12

commit v5 on v4

--- a/solution.py
+++ b/solution.py
@@ -1,3 +1,4 @@
+import collections
 import functools
 
 import jax
@@ -8,39 +9,60 @@
 from jax.sharding import PartitionSpec as P
 
 START = (
-    ("z_up", 0),
     ("z_down", 0),
     ("z_down", 1),
+    ("z_up", 0),
+    ("z_down", 2),
+    ("z_up", 1),
     ("a", 0),
-    ("z_up", 1),
+    ("z_up", 2),
     ("a", 1),
-    ("z_up", 2),
+    ("z_up", 3),
     ("pass_a", 0),
     ("b", 0),
-    ("z_down", 2),
+    ("z_down", 3),
     ("a", 2),
-    ("z_up", 3),
+    ("z_up", 4),
     ("pass_a", 1),
     ("b", 1),
-    ("z_down", 3),
+    ("z_down", 4),
+    ("a", 3),
+    ("z_up", 5),
     ("pass_b", 0),
+    ("pass_a", 2),
+    ("b", 2),
+    ("z_down", 5),
+    ("a", 4),
+    ("z_up", 6),
+    ("pass_a", 3),
+    ("b", 3),
+    ("z_down", 6),
+    ("a", 5),
+    ("z_up", 7),
+    ("pass_b", 1),
+    ("z_down", 7),
     ("gather_a", 0),
+    ("gather_a", 1),
+    ("gather_a", 2),
 )
 ORDER = (
-    ("z_up", 4),
-    ("a", 3),
-    ("b", 2),
-    ("z_down", 4),
-    ("pass_b", 1),
-    ("pass_a", 2),
-    ("gather_a", 1),
+    ("z_up", 8),
+    ("a", 6),
+    ("b", 4),
+    ("z_down", 8),
+    ("pass_a", 4),
+    ("gather_a", 3),
+    ("pass_b", 2),
+    ("across", 0),
     ("gather_b", 0),
     ("columns", 0),
-    ("across", 0),
 )
 BLOCK = 256
 ROW_FRAGS = 8
 MESH = pl.DeviceIdType.MESH
+
+
+Part = collections.namedtuple("Part", "step half")
 
 
 def to_device(src, dst, send_sem, recv_sem, frag, aux):
@@ -162,25 +184,31 @@
         pl.semaphore_signal(barrier, inc=1, device_id={"frag": there, "aux": other}, device_id_type=MESH)
     pl.semaphore_wait(barrier, len(greeted))
 
-    def rows_of(who):
-        return pl.ds(pl.multiple_of(who * rows, 16), rows)
+    first_rows = -(-rows // 32) * 16
+
+    def own(s):
+        return pl.ds(0, first_rows) if s.half == 0 else pl.ds(first_rows, rows - first_rows)
+
+    def rows_of(who, s):
+        here = own(s)
+        return pl.ds(pl.multiple_of(who * rows + here.start, 16), here.size)
 
     def two_cols(s):
         return pl.ds(pl.multiple_of(s * 2 * vir, 128), 2 * vir)
 
     def z_copy(s):
         return to_device(
-            blocks.at[0, :, two_cols(s)], a_stage.at[s], z_send.at[s], z_recv.at[s], up * 2 + 1, aux
+            blocks.at[0, own(s), two_cols(s.step)], a_stage.at[s.step, own(s)], z_send.at[s.step, s.half], z_recv.at[s.step, s.half], up * 2 + 1, aux
         )
 
     def cand_copy(s, slot, n, there):
-        src = blocks.at[0, :, two_cols(s)]
+        src = blocks.at[0, own(s), two_cols(s.step)]
         if there is None:
-            return pltpu.make_async_copy(src, cand.at[slot, s], cand_recv.at[slot, s])
-        return to_device(src, cand.at[slot, s], cand_send.at[n, s], cand_recv.at[slot, s], there, aux)
+            return pltpu.make_async_copy(src, cand.at[slot, s.step, own(s)], cand_recv.at[slot, s.step, s.half])
+        return to_device(src, cand.at[slot, s.step, own(s)], cand_send.at[n, s.step, s.half], cand_recv.at[slot, s.step, s.half], there, aux)
 
     def cand_forward(s):
-        return to_device(cand.at[2, s], cand.at[1, s], cand_pass.at[s], cand_recv.at[1, s], sibling, aux)
+        return to_device(cand.at[2, s.step, own(s)], cand.at[1, s.step, own(s)], cand_pass.at[s.step, s.half], cand_recv.at[1, s.step, s.half], sibling, aux)
 
     def z_up(s):
         @pl.when(core == 1)
@@ -201,12 +229,12 @@
 
     def a_source(s, core_is, part):
         if core_is == 0:
-            return blocks.at[0, :, pl.ds(pl.multiple_of(s * 2 * vir + part * vir, 128), vir)]
-        return a_stage.at[s, :, pl.ds(part * vir, vir)]
+            return blocks.at[0, own(s), pl.ds(pl.multiple_of(s.step * 2 * vir + part * vir, 128), vir)]
+        return a_stage.at[s.step, own(s), pl.ds(part * vir, vir)]
 
     def a_own(s, core_is):
         return pltpu.make_async_copy(
-            a_source(s, core_is, core_is), a_half.at[s, rows_of(aux)], a_recv.at[0, s]
+            a_source(s, core_is, core_is), a_half.at[s.step, rows_of(aux, s)], a_recv.at[0, s.step, s.half]
         )
 
     def a_copy(s, core_is, part, kind):
@@ -214,20 +242,20 @@
         n = 0 if kind == 0 else 1 + part
         return to_device(
             a_source(s, core_is, part),
-            a_half.at[s, rows_of(aux)],
-            a_send.at[n, s],
-            a_recv.at[kind, s],
+            a_half.at[s.step, rows_of(aux, s)],
+            a_send.at[n, s.step, s.half],
+            a_recv.at[kind, s.step, s.half],
             there,
             other,
         )
 
     def a_forward(s):
-        here = a_half.at[s, rows_of(outer)]
-        return to_device(here, here, a_send.at[3, s], a_recv.at[3, s], frag, mate)
+        here = a_half.at[s.step, rows_of(outer, s)]
+        return to_device(here, here, a_send.at[3, s.step, s.half], a_recv.at[3, s.step, s.half], frag, mate)
 
     def a_landing(s, kind, who):
-        here = a_half.at[s, rows_of(who)]
-        return to_device(here, here, a_send.at[3, s], a_recv.at[kind, s], frag, mate)
+        here = a_half.at[s.step, rows_of(who, s)]
+        return to_device(here, here, a_send.at[3, s.step, s.half], a_recv.at[kind, s.step, s.half], frag, mate)
 
     def begin_a(s):
         for core_is in range(2):
@@ -249,33 +277,33 @@
                     a_copy(s, core_is, 1, 2).start()
 
     def b_round(s):
-        return to_device(b_other.at[s], relay.at[s], b_send.at[0, s], relay_recv.at[s], next_row, aux)
+        return to_device(b_other.at[s.step, own(s)], relay.at[s.step, own(s)], b_send.at[0, s.step, s.half], relay_recv.at[s.step, s.half], next_row, aux)
 
     def b_relay(s):
         return to_device(
-            relay.at[s], b_half.at[s, rows_of(aux)], b_send.at[2, s], b_recv.at[1, s], last_row, relay_to
+            relay.at[s.step, own(s)], b_half.at[s.step, rows_of(aux, s)], b_send.at[2, s.step, s.half], b_recv.at[1, s.step, s.half], last_row, relay_to
         )
 
     def b_outer(s):
         return to_device(
-            b_other.at[s], b_half.at[s, rows_of(aux)], b_send.at[0, s], b_recv.at[2, s], frag, outer
+            b_other.at[s.step, own(s)], b_half.at[s.step, rows_of(aux, s)], b_send.at[0, s.step, s.half], b_recv.at[2, s.step, s.half], frag, outer
         )
 
     def b_through(s):
-        return to_device(b_mine.at[s], transit.at[s], b_send.at[1, s], b_recv.at[0, s], frag, outer)
+        return to_device(b_mine.at[s.step, own(s)], transit.at[s.step, own(s)], b_send.at[1, s.step, s.half], b_recv.at[0, s.step, s.half], frag, outer)
 
     def b_forward(s):
         return to_device(
-            transit.at[s], b_half.at[s, rows_of(outer)], b_send.at[1, s], b_recv.at[3, s], frag, mate
+            transit.at[s.step, own(s)], b_half.at[s.step, rows_of(outer, s)], b_send.at[1, s.step, s.half], b_recv.at[3, s.step, s.half], frag, mate
         )
 
     def b_landing(s, kind, who):
-        here = b_half.at[s, rows_of(who)]
-        return to_device(here, here, b_share.at[kind, s], b_recv.at[kind, s], sibling, aux)
+        here = b_half.at[s.step, rows_of(who, s)]
+        return to_device(here, here, b_share.at[kind, s.step, s.half], b_recv.at[kind, s.step, s.half], sibling, aux)
 
     def chosen(s, which):
         cols = pl.ds(pl.multiple_of(which * vir, 128), vir)
-        one, two, three = (cand[n, s, :, cols] for n in range(3))
+        one, two, three = (cand[n, s.step, own(s), cols] for n in range(3))
         chosen_at = off_scalars[0, 0, 0]
         return jnp.where(chosen_at == 1, one, jnp.where(chosen_at == 2, two, three))
 
@@ -293,18 +321,18 @@
             cand_copy(s, 2, 1, down * 2 + 1).wait_recv()
             cand_forward(s).wait_recv()
 
-        b_other[s] = chosen(s, 1 - q_half)
+        b_other[s.step, own(s), :] = chosen(s, 1 - q_half)
 
         @pl.when(member)
         def _():
             b_round(s).start()
-            b_half[s, rows_of(aux), :] = chosen(s, q_half)
+            b_half[s.step, rows_of(aux, s), :] = chosen(s, q_half)
             b_landing(s, 0, aux).start()
 
         @pl.when(stranger)
         def _():
             b_outer(s).start()
-            b_mine[s] = chosen(s, q_half)
+            b_mine[s.step, own(s), :] = chosen(s, q_half)
             b_through(s).start()
 
     def pass_a(s):
@@ -398,7 +426,7 @@
     for name, n in START:
         if (name, n) == ("b", 0):
             know_offsets()
-        stages[name](n)
+        stages[name](Part(n // 2, n % 2))
 
     @pl.when(member)
     def _():
@@ -497,10 +525,17 @@
 
     @pl.loop(0, steps)
     def _(s):
-        for name, lead in ORDER:
-            @pl.when(s + lead < steps)
-            def _():
-                stages[name](s + lead)
+        for half in range(2):
+            for name, lead in ORDER:
+                part = Part(s + (half + lead) // 2, (half + lead) % 2)
+                if name in ("columns", "across"):
+                    if part.half != (name == "columns"):
+                        continue
+                    part = part.step
+
+                @pl.when(s + (half + lead) // 2 < steps)
+                def _():
+                    stages[name](part)
 
     for n in range(1, 4):
         total[n, 2 * aux_rows :, :] = total[0, 2 * aux_rows :, :]
@@ -526,36 +561,37 @@
         landed[who] = total[aux]
 
     @pl.loop(0, steps)
-    def _(s):
-        cand_copy(s, 0, 0, sibling).wait_send()
-        cand_copy(s, 2, 1, sibling).wait_send()
-        a_forward(s).wait_send()
-        for core_is in range(2):
-            @pl.when(core == core_is)
+    def _(step):
+        for s in (Part(step, 0), Part(step, 1)):
+            cand_copy(s, 0, 0, sibling).wait_send()
+            cand_copy(s, 2, 1, sibling).wait_send()
+            a_forward(s).wait_send()
+            for core_is in range(2):
+                @pl.when(core == core_is)
+                def _():
+                    a_copy(s, core_is, 0, 1).wait_send()
+                    a_copy(s, core_is, 1, 1).wait_send()
+
+                    @pl.when(member)
+                    def _():
+                        a_copy(s, core_is, 1 - core_is, 0).wait_send()
+
+            @pl.when(core == 1)
             def _():
-                a_copy(s, core_is, 0, 1).wait_send()
-                a_copy(s, core_is, 1, 1).wait_send()
-
-                @pl.when(member)
-                def _():
-                    a_copy(s, core_is, 1 - core_is, 0).wait_send()
-
-        @pl.when(core == 1)
-        def _():
-            z_copy(s).wait_send()
-            cand_forward(s).wait_send()
-
-        @pl.when(member)
-        def _():
-            for kind, who_is in enumerate((aux, mate, outer, far)):
-                b_landing(s, kind, who_is).wait_send()
-
-        b_round(s).wait_send()
-        b_through(s).wait_send()
-
-        @pl.when(relays)
-        def _():
-            b_relay(s).wait_send()
+                z_copy(s).wait_send()
+                cand_forward(s).wait_send()
+
+            @pl.when(member)
+            def _():
+                for kind, who_is in enumerate((aux, mate, outer, far)):
+                    b_landing(s, kind, who_is).wait_send()
+
+            b_round(s).wait_send()
+            b_through(s).wait_send()
+
+            @pl.when(relays)
+            def _():
+                b_relay(s).wait_send()
 
     for n in range(1, 4):
         sum_copy(n).wait_send()
@@ -662,17 +698,17 @@
             pltpu.VMEM((3, 8, 128), jnp.int32),
             pltpu.SMEM((2, 8, 128), jnp.int32),
             dma((5,)),
-            dma((steps,)),
-            dma((steps,)),
-            dma((4, steps)),
-            dma((4, steps)),
-            dma((2, steps)),
-            dma((3, steps)),
-            dma((steps,)),
-            dma((3, steps)),
-            dma((4, steps)),
-            dma((4, steps)),
-            dma((steps,)),
+            dma((steps, 2)),
+            dma((steps, 2)),
+            dma((4, steps, 2)),
+            dma((4, steps, 2)),
+            dma((2, steps, 2)),
+            dma((3, steps, 2)),
+            dma((steps, 2)),
+            dma((3, steps, 2)),
+            dma((4, steps, 2)),
+            dma((4, steps, 2)),
+            dma((steps, 2)),
             dma((6,)),
             dma((4,)),
             dma((4,)),

time: 221 us -> 216 us (0.977)
  Pallas kernels: 217 us -> 212 us
    pallas_call x1, Pallas kernels: 217 us -> 212 us  [on_device(): pl.pallas_call(functools.partial(kernel, frag_total), out_shape=(jax.Shap...]
where the time goes in v5:
time: 216 us
  Pallas kernels  212 us (98%)
  between operations  2.98 us (1%)
    pallas_call x1, Pallas kernels, on_device(): pl.pallas_call(functools.partial(kernel, frag_total), out_shape=(jax.Shap...  212 us

profile of v5, /device:TPU:1, one launch (start us, length us, event | category | flops | bytes accessed | tf_op | source)
XLA Modules:
  0.0 216.1 jit_solution(15745832354623497173)
XLA Ops:
  1.3 211.7 %pair_terms.1 = (f32[1]{0:T(128)}, f32[1,64,256]{2,1,0:T(8,128)}, bf16[8,752,512]{2,1,0:T(8,128)(2,1)}, bf16[8,752,256]{2,1,0:T(8,128)(2,1)}, bf16[8,752,256]{2,1,0:T(8,128)(2,1)}) custom-call(bf16[1,752,4096]{2,1,0:T(8,128)(2,1)} %blocks.1, f32[16,32]{1,0:T(8,128)} %bitcast.1, f32[32,256]{1,0:T(8,128)} %vir_energy_in.1, s32[32]{0:T(128)} %occ_count_in.1, ...), custom_call_target="tpu_custom_call" | custom-call | flops 25232932864 | bytes 6160384 | tf_op jit(solution)/shard_map/pair_terms/pallas_call | solution.py:667
  213.5 1.5 copy.12

commit v6 on v5

--- a/solution.py
+++ b/solution.py
@@ -58,6 +58,7 @@
     ("columns", 0),
 )
 BLOCK = 256
+KEPT = 3
 ROW_FRAGS = 8
 MESH = pl.DeviceIdType.MESH
 
@@ -523,45 +524,7 @@
     stages["columns"] = columns
     stages["across"] = across
 
-    @pl.loop(0, steps)
-    def _(s):
-        for half in range(2):
-            for name, lead in ORDER:
-                part = Part(s + (half + lead) // 2, (half + lead) % 2)
-                if name in ("columns", "across"):
-                    if part.half != (name == "columns"):
-                        continue
-                    part = part.step
-
-                @pl.when(s + (half + lead) // 2 < steps)
-                def _():
-                    stages[name](part)
-
-    for n in range(1, 4):
-        total[n, 2 * aux_rows :, :] = total[0, 2 * aux_rows :, :]
-    who = q_half * 2 + core
-
-    def sum_copy(n):
-        column = lax.rem(aux + n, 4)
-        there = sibling if n == 0 else chip * 2 + pair
-        return to_device(total.at[column], landed.at[who], sum_send.at[n], sum_recv.at[who], there, column)
-
-    def sum_landing(n):
-        return to_device(landed.at[n], landed.at[n], sum_send.at[0], sum_recv.at[n], sibling, aux)
-
-    for n in (2, 1, 3):
-        sum_copy(n).start()
-
-    @pl.when(stranger)
-    def _():
-        sum_copy(0).start()
-
-    @pl.when(member)
-    def _():
-        landed[who] = total[aux]
-
-    @pl.loop(0, steps)
-    def _(step):
+    def drain(step):
         for s in (Part(step, 0), Part(step, 1)):
             cand_copy(s, 0, 0, sibling).wait_send()
             cand_copy(s, 2, 1, sibling).wait_send()
@@ -592,6 +555,52 @@
             @pl.when(relays)
             def _():
                 b_relay(s).wait_send()
+
+    @pl.loop(0, steps)
+    def _(s):
+        for half in range(2):
+            for name, lead in ORDER:
+                part = Part(s + (half + lead) // 2, (half + lead) % 2)
+                if (name, half) == ("gather_b", 0):
+                    @pl.when(s >= KEPT)
+                    def _():
+                        drain(s - KEPT)
+
+                if name in ("columns", "across"):
+                    if part.half != (name == "columns"):
+                        continue
+                    part = part.step
+
+                @pl.when(s + (half + lead) // 2 < steps)
+                def _():
+                    stages[name](part)
+
+    for n in range(1, 4):
+        total[n, 2 * aux_rows :, :] = total[0, 2 * aux_rows :, :]
+    who = q_half * 2 + core
+
+    def sum_copy(n):
+        column = lax.rem(aux + n, 4)
+        there = sibling if n == 0 else chip * 2 + pair
+        return to_device(total.at[column], landed.at[who], sum_send.at[n], sum_recv.at[who], there, column)
+
+    def sum_landing(n):
+        return to_device(landed.at[n], landed.at[n], sum_send.at[0], sum_recv.at[n], sibling, aux)
+
+    for n in (2, 1, 3):
+        sum_copy(n).start()
+
+    @pl.when(stranger)
+    def _():
+        sum_copy(0).start()
+
+    @pl.when(member)
+    def _():
+        landed[who] = total[aux]
+
+    @pl.loop(steps - KEPT, steps)
+    def _(step):
+        drain(step)
 
     for n in range(1, 4):
         sum_copy(n).wait_send()

time: 216 us -> 216 us (level)
  no operation moved by 1% of the time
where the time goes in v6:
time: 216 us
  Pallas kernels  212 us (98%)
  between operations  2.98 us (1%)
    pallas_call x1, Pallas kernels, on_device(): pl.pallas_call(functools.partial(kernel, frag_total), out_shape=(jax.Shap...  212 us

profile of v6, /device:TPU:1, one launch (start us, length us, event | category | flops | bytes accessed | tf_op | source)
XLA Modules:
  0.0 216.2 jit_solution(8404728385014153798)
XLA Ops:
  1.3 211.7 %pair_terms.1 = (f32[1]{0:T(128)}, f32[1,64,256]{2,1,0:T(8,128)}, bf16[8,752,512]{2,1,0:T(8,128)(2,1)}, bf16[8,752,256]{2,1,0:T(8,128)(2,1)}, bf16[8,752,256]{2,1,0:T(8,128)(2,1)}) custom-call(bf16[1,752,4096]{2,1,0:T(8,128)(2,1)} %blocks.1, f32[16,32]{1,0:T(8,128)} %bitcast.1, f32[32,256]{1,0:T(8,128)} %vir_energy_in.1, s32[32]{0:T(128)} %occ_count_in.1, ...), custom_call_target="tpu_custom_call" | custom-call | flops 25232932864 | bytes 6160384 | tf_op jit(solution)/shard_map/pair_terms/pallas_call | solution.py:676
  213.6 1.5 copy.12
